TPU v7x, 128 devices: a whole 4x4x4 slice. The times are simulated.
128 devices in a mesh: pb: 64 (over y, x, z), ha: 2 (over core).
Axes of the slice: x: 4, y: 4, z: 4, core: 2. Of those that a mesh axis runs over, the one named last changes fastest.
Arguments:
- tokens: bfloat16 [65536, 768], P('pb')
- shift_attn: float32 [768], replicated, may hold values from -3 to 3
- scale_attn: float32 [768], replicated, may hold values from -3 to 3
- gate_attn: float32 [768], replicated, may hold values from 0.5 to 2
- shift_mlp: float32 [768], replicated, may hold values from -3 to 3
- scale_mlp: float32 [768], replicated, may hold values from -3 to 3
- gate_mlp: float32 [768], replicated, may hold values from 0.5 to 2
- w_query: bfloat16 [768, 768], P(None, 'ha')
- w_key: bfloat16 [768, 768], P(None, 'ha')
- w_value: bfloat16 [768, 768], P(None, 'ha'), may hold values from -0.875 to 0.875
- w_out: bfloat16 [768, 768], P('ha'), may hold values from -0.21875 to 0.21875
- w_fc1: bfloat16 [768, 3072], P(None, 'ha'), may hold values from -0.21875 to 0.21875
- w_fc2: bfloat16 [3072, 768], P('ha'), may hold values from -0.109375 to 0.109375
- contact_owner: int32 [512, 8], replicated, may hold values from 0 to 63, all different within a row; in each aligned block of 8 rows (0 to 7, 8 to 15, ...) at most 2 rows name the same one
- contact_local: int32 [512, 8], replicated, may hold values from 0 to 7
- contact_count: int32 [512], P('pb'), may hold values from 1 to 8
Outputs:
- block_output: bfloat16 [65536, 768], P(('pb', 'ha'))
Inputs may be any that keep to these rules, and one draw needn't show every extreme that they name: `contact_owner`: each query block lists 8 different owners. Among the 8 query blocks of one index of pb (aligned blocks of rows), no owner is named by more than 2 of them, a bound that some block reaches.
All inputs are finite; a program needn't handle non-finite values.
Results may differ from a plain program's by a relative error of at most 0.017.
Values may be sent and summed in bfloat16 or wider, within the bound.
A program may use at most 192 MiB of HBM per device.

v0:
```python
import jax
import jax.numpy as jnp
from jax import lax
from jax.sharding import PartitionSpec as P

D = 768
HEADS = 16
QBLK = 128
KT = 8
QB_DEV = 8


epsilon = 1e-06


def modulate(stream, shift, scale):
    center = stream - jnp.mean(stream, -1, keepdims=True)
    spread = jnp.mean(center * center, -1, keepdims=True)
    return center * lax.rsqrt(spread + epsilon) * (1.0 + scale) + shift


def attend(operands, head_dim):
    queries, key_rows, value_rows, live_mask = operands
    group_count, row_count, col_count = queries.shape
    head_count = col_count // head_dim
    query_heads = queries.reshape(group_count, row_count, head_count, head_dim)
    key_heads = key_rows.reshape(group_count, -1, head_count, head_dim)
    value_heads = value_rows.reshape(group_count, -1, head_count, head_dim)
    scores = jnp.einsum(
        "gihd,gjhd->ghij", query_heads, key_heads, preferred_element_type=jnp.float32
    ) * head_dim ** (-0.5)
    scores = jnp.where(live_mask[:, None, None, :], scores, -1e30)
    row_max = jnp.max(scores, -1, keepdims=True)
    weights = jnp.exp(scores - row_max)
    totals = jnp.sum(weights, -1)
    outputs = jnp.einsum(
        "ghij,gjhd->gihd",
        weights.astype(jnp.bfloat16),
        value_heads,
        preferred_element_type=jnp.float32,
    )
    outputs = outputs / jnp.transpose(totals, (0, 2, 1))[..., None]
    return outputs.astype(jnp.bfloat16).reshape(group_count, row_count, col_count)


def shards(
    tokens,
    shift_attn,
    scale_attn,
    gate_attn,
    shift_mlp,
    scale_mlp,
    gate_mlp,
    w_query,
    w_key,
    w_value,
    w_out,
    w_fc1,
    w_fc2,
    contact_owner,
    contact_local,
    contact_count,
):
    pb_count = lax.axis_size("pb")
    ha_count = lax.axis_size("ha")
    my_pb = lax.axis_index("pb")
    my_ha = lax.axis_index("ha")
    head_dim = D // HEADS
    head_cols = w_query.shape[1]
    blocks = QB_DEV
    tile_rows = QBLK
    link_count = KT
    slot_count = 2 * max(1, (blocks * link_count + 2 * pb_count - 1) // (2 * pb_count))
    stream = tokens.astype(jnp.float32)
    normed = modulate(stream, shift_attn, scale_attn).astype(jnp.bfloat16)
    queries = jnp.dot(normed, w_query, preferred_element_type=jnp.float32).astype(jnp.bfloat16)
    key_part = jnp.dot(normed, w_key, preferred_element_type=jnp.float32).astype(jnp.bfloat16)
    value_part = jnp.dot(normed, w_value, preferred_element_type=jnp.float32).astype(jnp.bfloat16)
    local_kv = jnp.concatenate([key_part, value_part], 1).reshape(blocks, tile_rows, 2 * head_cols)
    owner_table = contact_owner.reshape(pb_count, blocks, link_count)
    local_table = contact_local.reshape(pb_count, blocks, link_count)
    peer_ids = jnp.arange(pb_count, dtype=jnp.int32)
    my_owners = lax.dynamic_index_in_dim(owner_table, my_pb, 0, keepdims=False)
    hit_table = (my_owners[:, :, None] == peer_ids[None, None, :]).astype(jnp.int32)
    named_count = jnp.sum(hit_table, 1)
    earlier = jnp.cumsum(named_count, 0) - named_count
    entry_slot = jnp.sum(hit_table * earlier[:, None, :], -1)
    entry_index = (my_owners * slot_count + entry_slot).reshape(-1)
    hit_mine = (owner_table == my_pb).astype(jnp.int32)
    wanted = jnp.sum(hit_mine, -1)
    slot_rank = jnp.cumsum(wanted, 1) - wanted
    which_block = jnp.sum(hit_mine * local_table, -1)
    slot_ids = jnp.arange(slot_count, dtype=jnp.int32)
    chooser = wanted[:, None, :] * (slot_rank[:, None, :] == slot_ids[None, :, None]).astype(
        jnp.int32
    )
    send_block = jnp.sum(chooser * which_block[:, None, :], -1)
    outgoing = jnp.take(local_kv, send_block.reshape(-1), axis=0)
    incoming = lax.all_to_all(outgoing, "pb", split_axis=0, concat_axis=0, tiled=True)
    fetched = jnp.take(incoming, entry_index, axis=0)
    fetched = fetched.reshape(blocks, link_count, tile_rows, 2 * head_cols)
    all_kv = jnp.concatenate([local_kv[:, None], fetched], 1).reshape(
        blocks, (1 + link_count) * tile_rows, 2 * head_cols
    )
    tile_order = jnp.arange(1 + link_count, dtype=jnp.int32)
    live_tiles = (tile_order[None, :] == 0) | (tile_order[None, :] - 1 < contact_count[:, None])
    live_mask = jnp.repeat(live_tiles, tile_rows, axis=1)
    group_size = 4
    group_total = blocks // group_size
    query_groups = queries.reshape(group_total, group_size, tile_rows, head_cols)
    kv_groups = all_kv.reshape(group_total, group_size, -1, 2 * head_cols)
    mask_groups = live_mask.reshape(group_total, group_size, -1)

    def attend_group(operands):
        query_rows, kv_rows, mask_rows = operands
        return attend(
            (query_rows, kv_rows[..., :head_cols], kv_rows[..., head_cols:], mask_rows), head_dim
        )

    attention = lax.map(attend_group, (query_groups, kv_groups, mask_groups)).reshape(
        blocks * tile_rows, head_cols
    )
    seq_rows = blocks * tile_rows
    out_count = seq_rows // ha_count
    proj_own = lax.psum_scatter(
        jnp.dot(attention, w_out, preferred_element_type=jnp.float32).astype(jnp.bfloat16),
        "ha",
        scatter_dimension=0,
        tiled=True,
    ).astype(jnp.float32)
    stream_own = lax.dynamic_slice_in_dim(stream, my_ha * out_count, out_count, 0)
    resid_own = (stream_own + gate_attn * proj_own).astype(jnp.bfloat16)
    residual = lax.all_gather(resid_own, "ha", axis=0, tiled=True)
    normed_mlp = modulate(residual.astype(jnp.float32), shift_mlp, scale_mlp).astype(jnp.bfloat16)
    hidden = jax.nn.gelu(
        jnp.dot(normed_mlp, w_fc1, preferred_element_type=jnp.float32), approximate=True
    ).astype(jnp.bfloat16)
    mlp_own = lax.psum_scatter(
        jnp.dot(hidden, w_fc2, preferred_element_type=jnp.float32).astype(jnp.bfloat16),
        "ha",
        scatter_dimension=0,
        tiled=True,
    ).astype(jnp.float32)
    return (resid_own.astype(jnp.float32) + gate_mlp * mlp_own).astype(jnp.bfloat16)


def solution(mesh):
    placed = (
        P("pb", None),
        P(),
        P(),
        P(),
        P(),
        P(),
        P(),
        P(None, "ha"),
        P(None, "ha"),
        P(None, "ha"),
        P("ha", None),
        P(None, "ha"),
        P("ha", None),
        P(),
        P(),
        P("pb"),
    )
    return jax.shard_map(
        shards, mesh=mesh, in_specs=placed, out_specs=P(("pb", "ha"), None), check_vma=False
    )
```

profile of v0, /device:TPU:1, one launch (start us, length us, event | category | flops | bytes accessed | tf_op | source)
XLA Modules:
  0.0 735.9 jit_solution(15916799097382627914)
XLA Ops:
  6.5 0.9 convert_reduce_fusion.3
  8.5 1.8 convert_reduce_fusion.1
  10.3 2.0 multiply_reduce_fusion
  12.4 0.6 add_convert_fusion
  13.1 0.8 convolution_convert_fusion.2
  13.9 0.8 convolution_convert_fusion.3
  14.8 1.3 pad_maximum_fusion.1
  16.0 2.6 copy.38
  18.7 12.1 %gather_fusion = bf16[128,128,768]{2,1,0:T(8,128)(2,1)} fusion(bf16[8,128,768]{2,1,0:T(8,128)(2,1)} %bitcast.63, s32[1024]{0:T(1024)S(1)} %pad_clamp_fusion.1), kind=kCustom, calls=%fused_computation | custom fusion | bytes 50332160 | tf_op jit(solution)/shard_map/jit(_take)/gather | solution.py:98
  30.8 21.3 %broadcast_select_fusion = bf16[128,128,768]{2,1,0:T(8,128)(2,1)} fusion(bf16[128,128,768]{2,1,0:T(8,128)(2,1)} %gather_fusion, pred[128]{0:T(512)(128)(4,1)S(1)} %compare_and_fusion.1), kind=kLoop, calls=%fused_computation.16 | loop fusion | flops 12582912 | bytes 50331776 | tf_op jit(solution)/shard_map/jit(_take)/select_n | solution.py:98
  52.1 12.3 %all-to-all-start = ((bf16[128,128,768]{2,1,0:T(8,128)(2,1)}), bf16[128,128,768]{2,1,0:T(8,128)(2,1)}, u32[]{:S(2)}, u32[]{:S(2)}) async-start(bf16[128,128,768]{2,1,0:T(8,128)(2,1)} %broadcast_select_fusion), calls=%async_computation | async-start | bytes 50331648 | tf_op jit(solution)/shard_map/all_to_all | solution.py:99
  64.7 0.3 select_reduce_fusion
  65.5 3.4 convolution_convert_fusion.1
  68.9 440.4 %all-to-all-done = bf16[128,128,768]{2,1,0:T(8,128)(2,1)} async-done(((bf16[128,128,768]{2,1,0:T(8,128)(2,1)}), bf16[128,128,768]{2,1,0:T(8,128)(2,1)}, u32[]{:S(2)}, u32[]{:S(2)}) %all-to-all-start) | async-done | bytes 25165856 | tf_op jit(solution)/shard_map/all_to_all | solution.py:99
  509.3 15.5 %gather_fusion.1 = bf16[64,128,768]{2,1,0:T(8,128)(2,1)} fusion(bf16[128,128,768]{2,1,0:T(8,128)(2,1)} %all-to-all-done, s32[1024]{0:T(1024)S(1)} %pad_clamp_fusion), kind=kCustom, calls=%fused_computation.1 | custom fusion | bytes 25166080 | tf_op jit(solution)/shard_map/jit(_take)/gather | solution.py:100
  524.8 6.6 broadcast_select_fusion.1
  531.4 6.1 pad_maximum_fusion
  537.5 115.3 %while.10 = (s32[]{:T(128)}, bf16[2,4,128,384]{3,2,1,0:T(8,128)(2,1)}, bf16[2,4,1152,768]{3,2,1,0:T(8,128)(2,1)}, pred[2,4,1152]{2,1,0:T(4,128)(4,1)S(1)}, bf16[2,4,128,384]{3,2,1,0:T(8,128)(2,1)}, /*index=5*/s32[]{:T(128)}) while((s32[]{:T(128)}, bf16[2,4,128,384]{3,2,1,0:T(8,128)(2,1)}, bf16[2,4,1152,768]{3,2,1,0:T(8,128)(2,1)}, ...), condition=%wide.region_12.13_spmd, body=%wide.region_9.12_spmd.sunk | while | flops 939384832 | bytes 110196816 | solution.py:120
  537.5 6.4 constant_dynamic-slice_fusion.4
  543.9 10.5 %copy.47 = bf16[1,4,1152,768]{2,3,1,0:T(8,128)(2,1)} copy(bf16[1,4,1152,768]{3,2,1,0:T(8,128)(2,1)} %constant_dynamic-slice_fusion.4) | data formatting | bytes 14155776 | tf_op jit(solution)/shard_map/while/body/jit(dynamic_index_in_dim)/dynamic_slice | solution.py:120
  554.4 6.5 fusion.77
  560.9 1.0 constant_dynamic-slice_fusion.5
  562.0 0.2 copy.48
  562.2 11.3 %fusion.78 = (f32[4,8,128]{2,1,0:T(8,128)S(1)}, f32[4,8,128,1152]{3,2,1,0:T(8,128)}) fusion(bf16[4,128,8,48]{1,3,2,0:T(8,128)(2,1)S(1)} %bitcast.69, bf16[4,1152,8,48]{1,3,2,0:T(8,128)(2,1)} %bitcast.66, pred[4,1152]{1,0:T(4,128)(4,1)S(1)} %dynamic-slice_bitcast_fusion.3), kind=kOutput, calls=%fused_computation.87.clone.1 | convolution fusion | flops 467136512 | bytes 22827520 | tf_op jit(solution)/shard_map/while/body/eval_jaxpr/gihd,gjhd->ghij/dot_general | solution.py:29
  573.6 9.3 %fusion.79 = f32[4,8,128]{2,1,0:T(8,128)S(1)} fusion(f32[4,8,128,1152]{3,2,1,0:T(8,128)} %get-tuple-element.103, f32[4,8,128]{2,1,0:T(8,128)S(1)} %get-tuple-element.104), kind=kLoop, calls=%fused_computation.5.clone.1 | loop fusion | flops 9433088 | bytes 18907136 | tf_op jit(solution)/shard_map/while/body/eval_jaxpr/reduce_sum | solution.py:35
  582.9 11.3 %fusion.80 = bf16[4,128,8,48]{1,3,2,0:T(8,128)(2,1)S(1)} fusion(bf16[4,1152,8,48]{1,3,2,0:T(8,128)(2,1)} %bitcast.65, f32[4,8,128,1152]{3,2,1,0:T(8,128)} %get-tuple-element.103, f32[4,8,128]{2,1,0:T(8,128)S(1)} %get-tuple-element.104, f32[4,128,8]{1,2,0:T(8,128)S(1)} %bitcast.71), kind=kOutput, calls=%fused_computation.11.clone.1 | convolution fusion | flops 462815232 | bytes 22839296 | tf_op jit(solution)/shard_map/while/body/eval_jaxpr/ghij,gjhd->gihd/dot_general | solution.py:36
  594.2 0.2 copy.49
  594.4 0.8 constant_dynamic-update-slice_fusion.2
  595.2 6.4 constant_dynamic-slice_fusion.4
  601.6 10.5 %copy.47 = bf16[1,4,1152,768]{2,3,1,0:T(8,128)(2,1)} copy(bf16[1,4,1152,768]{3,2,1,0:T(8,128)(2,1)} %constant_dynamic-slice_fusion.4) | data formatting | bytes 14155776 | tf_op jit(solution)/shard_map/while/body/jit(dynamic_index_in_dim)/dynamic_slice | solution.py:120
  612.1 6.5 fusion.77
  618.6 1.0 constant_dynamic-slice_fusion.5
  619.6 0.2 copy.48
  619.9 11.3 %fusion.78 = (f32[4,8,128]{2,1,0:T(8,128)S(1)}, f32[4,8,128,1152]{3,2,1,0:T(8,128)}) fusion(bf16[4,128,8,48]{1,3,2,0:T(8,128)(2,1)S(1)} %bitcast.69, bf16[4,1152,8,48]{1,3,2,0:T(8,128)(2,1)} %bitcast.66, pred[4,1152]{1,0:T(4,128)(4,1)S(1)} %dynamic-slice_bitcast_fusion.3), kind=kOutput, calls=%fused_computation.87.clone.1 | convolution fusion | flops 467136512 | bytes 22827520 | tf_op jit(solution)/shard_map/while/body/eval_jaxpr/gihd,gjhd->ghij/dot_general | solution.py:29
  631.2 9.3 %fusion.79 = f32[4,8,128]{2,1,0:T(8,128)S(1)} fusion(f32[4,8,128,1152]{3,2,1,0:T(8,128)} %get-tuple-element.103, f32[4,8,128]{2,1,0:T(8,128)S(1)} %get-tuple-element.104), kind=kLoop, calls=%fused_computation.5.clone.1 | loop fusion | flops 9433088 | bytes 18907136 | tf_op jit(solution)/shard_map/while/body/eval_jaxpr/reduce_sum | solution.py:35
  640.6 11.3 %fusion.80 = bf16[4,128,8,48]{1,3,2,0:T(8,128)(2,1)S(1)} fusion(bf16[4,1152,8,48]{1,3,2,0:T(8,128)(2,1)} %bitcast.65, f32[4,8,128,1152]{3,2,1,0:T(8,128)} %get-tuple-element.103, f32[4,8,128]{2,1,0:T(8,128)S(1)} %get-tuple-element.104, f32[4,128,8]{1,2,0:T(8,128)S(1)} %bitcast.71), kind=kOutput, calls=%fused_computation.11.clone.1 | convolution fusion | flops 462815232 | bytes 22839296 | tf_op jit(solution)/shard_map/while/body/eval_jaxpr/ghij,gjhd->gihd/dot_general | solution.py:36
  652.1 0.8 constant_dynamic-update-slice_fusion.2
  652.9 3.4 convolution_convert_fusion
  656.3 0.3 all-gather.2.cloned.1.call-start
  656.6 3.3 convert_element_type.59
  659.9 24.6 %reduce-scatter.3.cloned.1.call-done = bf16[512,768]{1,0:T(8,128)(2,1)} async-done(((bf16[1024,768]{1,0:T(8,128)(2,1)}), bf16[512,768]{1,0:T(8,128)(2,1)}) %reduce-scatter.3.cloned.1.call-update) | async-done | bytes 786448 | tf_op jit(solution)/shard_map/reduce_scatter | solution.py:125
  684.5 2.7 add_convert_fusion.2
  687.3 14.0 %all-gather.2.cloned.1.call-done = bf16[1024,768]{1,0:T(8,128)(2,1)} async-done(((bf16[512,768]{1,0:T(8,128)(2,1)}), bf16[1024,768]{1,0:T(8,128)(2,1)}) %all-gather.2.cloned.1.call-update) | async-done | bytes 1572880 | tf_op jit(solution)/shard_map/all_gather | solution.py:133
  701.3 1.7 convert_reduce_fusion
  703.0 2.0 fusion.25
  705.1 8.8 %fusion.31 = bf16[1024,768]{1,0:T(8,128)(2,1)} fusion(bf16[1536,768]{1,0:T(8,128)(2,1)S(1)} %copy-done, bf16[768,1536]{1,0:T(8,128)(2,1)} %param.29, bf16[1024,768]{1,0:T(8,128)(2,1)} %all-gather.2.cloned.1.call-done, f32[768]{0:T(1024)S(1)} %copy-done.14, f32[768]{0:T(1024)S(1)} %broadcast_add_fusion, f32[1024]{0:T(1024)S(1)} %add_rsqrt_fusion, ...), kind=kOutput, calls=%fused_computation.41 | convolution fusion | flops 4851499008 | bytes 7878656 | tf_op jit(solution)/shard_map/dot_general | solution.py:139
  713.9 13.2 %reduce-scatter.5.cloned.1.call-done = bf16[512,768]{1,0:T(8,128)(2,1)} async-done(((bf16[1024,768]{1,0:T(8,128)(2,1)}), bf16[512,768]{1,0:T(8,128)(2,1)}) %reduce-scatter.5.cloned.1.call-update) | async-done | bytes 786448 | tf_op jit(solution)/shard_map/reduce_scatter | solution.py:138
  727.1 2.2 add_convert_fusion.1
  (74 shorter events, 2.1 us)
Async XLA Ops:
  6.5 698.5 %copy-start = (bf16[1536,768]{1,0:T(8,128)(2,1)S(1)}, bf16[1536,768]{1,0:T(8,128)(2,1)}, u32[]{:S(2)}) copy-start(bf16[1536,768]{1,0:T(8,128)(2,1)} %param.30) | copy-start | bytes 7077892
  6.5 5.8 copy-start.9
  6.5 5.8 copy-start.6
  8.4 4.0 copy-start.2
  8.5 4.6 copy-start.12
  12.4 1.5 copy-start.13
  13.0 1.7 copy-start.4
  52.1 12.4 %copy-start.5 = (s32[512,8]{0,1:T(8,128)S(1)}, s32[512,8]{0,1:T(8,128)}, u32[]{:S(2)}) copy-start(s32[512,8]{0,1:T(8,128)} %param.31) | copy-start | bytes 49156
  52.1 13.1 %copy-start.11 = (s32[8]{0:T(128)S(1)}, s32[8]{0:T(128)}, u32[]{:S(2)}) copy-start(s32[8]{0:T(128)} %param.33) | copy-start | bytes 100
  52.1 457.2 %all-to-all-start = ((bf16[128,128,768]{2,1,0:T(8,128)(2,1)}), bf16[128,128,768]{2,1,0:T(8,128)(2,1)}, u32[]{:S(2)}, u32[]{:S(2)}) async-start(bf16[128,128,768]{2,1,0:T(8,128)(2,1)} %broadcast_select_fusion), calls=%async_computation | async-start | bytes 50331648 | tf_op jit(solution)/shard_map/all_to_all | solution.py:99
  64.4 620.1 %reduce-scatter.3.cloned.1.call-start = ((), (), s32[]{:S(2)}) async-start(), calls=%async_computation.3 | async-start | bytes 2359296 | tf_op jit(solution)/shard_map/reduce_scatter | solution.py:125
  524.8 6.6 copy-start.1
  656.3 28.2 %copy-start.7 = (f32[768]{0:T(1024)S(1)}, f32[768]{0:T(1024)}, u32[]{:S(2)}) copy-start(f32[768]{0:T(1024)} %param.21) | copy-start | bytes 9220
  656.3 45.0 %all-gather.2.cloned.1.call-start = ((), (), s32[]{:S(2)}) async-start(), calls=%async_computation.4 | async-start | bytes 2359296 | tf_op jit(solution)/shard_map/all_gather | solution.py:133
  659.9 27.4 %copy-start.10 = (f32[768]{0:T(1024)S(1)}, f32[768]{0:T(1024)}, u32[]{:S(2)}) copy-start(f32[768]{0:T(1024)} %param.23) | copy-start | bytes 9220
  659.9 45.2 %copy-start.14 = (f32[768]{0:T(1024)S(1)}, f32[768]{0:T(1024)}, u32[]{:S(2)}) copy-start(f32[768]{0:T(1024)} %param.22) | copy-start | bytes 9220
  687.2 39.9 %reduce-scatter.5.cloned.1.call-start = ((), (), s32[]{:S(2)}) async-start(), calls=%async_computation.5 | async-start | bytes 2359296 | tf_op jit(solution)/shard_map/reduce_scatter | solution.py:138
  705.1 22.1 %copy-start.3 = (bf16[512,768]{1,0:T(8,128)(2,1)S(1)}, bf16[512,768]{1,0:T(8,128)(2,1)}, u32[]{:S(2)}) copy-start(bf16[512,768]{1,0:T(8,128)(2,1)} %add_convert_fusion.2) | copy-start | bytes 2359300
  705.1 22.1 %copy-start.8 = (f32[768]{0:T(1024)S(1)}, f32[768]{0:T(1024)}, u32[]{:S(2)}) copy-start(f32[768]{0:T(1024)} %param.24) | copy-start | bytes 9220
Sparse Core Ops, SparseCore 0:
  656.4 28.0 reduce-scatter.2
  687.3 13.9 all-gather.1
  714.1 13.0 reduce-scatter.4
where the time goes:
time: 737 us; the launch traced here: 736 us
  waiting for transfers between devices  492 us (67%)
  local copies, waits for them, and re-layouts  82.8 us (11%)
  other arithmetic  72 us (10%)
  matrix products  62.6 us (8%)
  between operations  13.5 us (2%)
  starting transfers between devices  12.7 us (2%)
    all_to_all x1, waiting for transfers between devices, shards(): lax.all_to_all(outgoing, 'pb', split_axis=0, concat_axis=0, tiled=True)  440 us
    dynamic_slice x8, local copies, waits for them, and re-layouts, shards(): lax.map(attend_group, (query_groups, kv_groups, mask_groups))  36.4 us
    reduce_scatter x1, waiting for transfers between devices, shards(): lax.psum_scatter(jnp.dot(attention, w_out, preferred_element_type=jnp.flo...  24.6 us
    dot_general x2, matrix products, attend(): jnp.einsum('gihd,gjhd->ghij', query_heads, key_heads, preferred_element_t...  22.7 us
    dot_general x2, matrix products, attend(): jnp.einsum('ghij,gjhd->gihd', weights.astype(jnp.bfloat16), value_heads,...  22.5 us
    select_n x2, other arithmetic, shards(): outgoing = jnp.take(local_kv, send_block.reshape(-1), axis=0)  21.3 us
    reduce_sum x2, other arithmetic, attend(): totals = jnp.sum(weights, -1)  18.6 us
    gather x1, local copies, waits for them, and re-layouts, shards(): fetched = jnp.take(incoming, entry_index, axis=0)  15.5 us
  transfers between devices with their start and end apart: 4, of which 4 were waited for; matrix products, arithmetic and copies ran while one was open for 1% of the time, Pallas kernels for 0%

commit v1 on v0

v1 whole, which is shorter than its diff:
```python
import jax
import jax.numpy as jnp
from jax import lax
from jax.experimental import pallas as pl
from jax.experimental.pallas import tpu as pltpu
from jax.sharding import PartitionSpec as P

D = 768
HEADS = 16
HDIM = 48
FF = 3072
QBLK = 128
KT = 8
QB_DEV = 8
N_PB = 64
SIDE = 4
HALF = QBLK // 2
PART = D // 3
GRP = D // 2
MIB = 2**20
MESH = pl.DeviceIdType.MESH

ORDERS = ((2, 1, 0), (1, 0, 2), (0, 2, 1))
STRIDES = (16, 4, 1)
OFFS = (0, 1, 3, 2)

epsilon = 1e-06


def modulate(stream, shift, scale):
    center = stream - jnp.mean(stream, -1, keepdims=True)
    spread = jnp.mean(center * center, -1, keepdims=True)
    return center * lax.rsqrt(spread + epsilon) * (1.0 + scale) + shift


def exchange_kernel(
    tokens_ref, shift_ref, scale_ref, sel_ref, *refs
):
    w_in = refs[0:6]
    kv_ref = refs[6]
    w_out = refs[7:13]
    rows = [refs[13 + 4 * p : 17 + 4 * p] for p in range(3)]
    picked = refs[25]
    (a_s, a_r, af_s, af_r, b_s, b_r, bf_s, bf_r, c_s, c_r, x_s, x_r, l_s, w_s, w_r, wl_s) = refs[26:]

    pb = lax.axis_index("pb")
    ha = lax.axis_index("ha")
    me = (pb // 16, (pb // 4) % 4, pb % 4)

    def moved(base, axis, off):
        return base + (lax.rem(me[axis] + off, SIDE) - me[axis]) * STRIDES[axis]

    def chip(axis, off):
        return {"pb": moved(pb, axis, off), "ha": ha}

    other = {"pb": pb, "ha": 1 - ha}

    def remote(src, dst, ssem, rsem, dev):
        return pltpu.make_async_remote_copy(
            src_ref=src, dst_ref=dst, send_sem=ssem, recv_sem=rsem, device_id=dev, device_id_type=MESH
        )

    def norm_tile(t, carry):
        x = tokens_ref[pl.ds(pl.multiple_of(t * QBLK + ha * HALF, HALF), HALF), :].astype(jnp.float32)
        n = modulate(x, shift_ref[...], scale_ref[...]).astype(jnp.bfloat16)
        for p in range(3):
            rows[p][0][0, t] = n[:, p * PART : (p + 1) * PART]
        return carry

    barrier = pltpu.get_barrier_semaphore()
    for axis in range(3):
        for off in (1, 2, 3):
            pl.semaphore_signal(barrier, 1, device_id=chip(axis, off), device_id_type=MESH)
    pl.semaphore_signal(barrier, 1, device_id=other, device_id_type=MESH)
    lax.fori_loop(0, QB_DEV, norm_tile, 0)
    pl.semaphore_wait(barrier, 10)

    started = []

    def go(copy):
        copy.start()
        started.append(copy)

    local = []

    def send_a(p, d):
        a = ORDERS[p][0]
        return remote(
            rows[p][0].at[0], rows[p][0].at[3 if d == 0 else 1], a_s.at[p, d], a_r.at[p, d], chip(a, 1 if d == 0 else 3)
        )

    def forward_a(p, d):
        a = ORDERS[p][0]
        part = pl.ds(4 * d, 4)
        return remote(
            rows[p][0].at[3 if d == 0 else 1, part],
            rows[p][0].at[2, part],
            af_s.at[p, d],
            af_r.at[p, d],
            chip(a, 1 if d == 0 else 3),
        )

    def send_b(p, da, d):
        b = ORDERS[p][1]
        return remote(
            rows[p][0].at[da],
            rows[p][3 if d == 0 else 1].at[da],
            b_s.at[p, da, d],
            b_r.at[p, da, d],
            chip(b, 1 if d == 0 else 3),
        )

    def forward_b(p, da, d):
        b = ORDERS[p][1]
        part = pl.ds(4 * d, 4)
        return remote(
            rows[p][3 if d == 0 else 1].at[da, part],
            rows[p][2].at[da, part],
            bf_s.at[p, da, d],
            bf_r.at[p, da, d],
            chip(b, 1 if d == 0 else 3),
        )

    def send_c(p, db, g):
        c = ORDERS[p][2]
        off = OFFS[g]
        return remote(
            picked.at[p, g, db],
            kv_ref.at[p, 0, SIDE - off, db],
            c_s.at[p, db, g],
            c_r.at[p, db, g],
            chip(c, off),
        )

    def cross(p, db, g):
        src = picked.at[p, 0, db] if g == 0 else kv_ref.at[p, 0, SIDE - OFFS[g], db]
        return remote(
            src, kv_ref.at[p, 1, (SIDE - OFFS[g]) % SIDE, db], x_s.at[p, db, g], x_r.at[p, db, g], other
        )

    def keep(p, db):
        return pltpu.make_async_copy(picked.at[p, 0, db], kv_ref.at[p, 0, 0, db], l_s.at[p, db])

    def select(p, db):
        a, b, c = ORDERS[p]
        for g in range(4):
            dest = moved(pb, c, OFFS[g])

            def pick(j, carry):
                da, k = j // 2, j % 2
                owner = moved(moved(pb, b, db), a, da)
                code = sel_ref[dest, owner]
                number = jnp.where(k == 0, code & 7, (code >> 9) & 7)
                picked[p, g, db, j] = rows[p][db][da, number]
                return carry

            lax.fori_loop(0, 8, pick, 0)
        for g in (3, 1, 2):
            go(send_c(p, db, g))
        local.append(keep(p, db))
        local[-1].start()
        go(cross(p, db, 0))

    def relay(p, db):
        for g in (1, 2, 3):
            send_c(p, db, g).wait_recv()
            go(cross(p, db, g))

    for p in range(3):
        for d in range(2):
            go(send_a(p, d))
    for p in range(3):
        for d in range(2):
            go(send_b(p, 0, d))
    weights = [remote(w_in[i], w_out[i].at[ha], w_s.at[i], w_r.at[i], other) for i in range(6)]
    kept = [pltpu.make_async_copy(w_in[i], w_out[i].at[ha], wl_s.at[i]) for i in range(6)]
    for copy in weights:
        go(copy)
    for copy in kept:
        local.append(copy)
        copy.start()
    for p in range(3):
        for d in range(2):
            send_a(p, d).wait_recv()
            go(forward_a(p, d))
        for d in range(2):
            for da in (3, 1):
                go(send_b(p, da, d))
    for p in range(3):
        for d in range(2):
            forward_a(p, d).wait_recv()
        for d in range(2):
            go(send_b(p, 2, d))
    for da in (0, 3, 1, 2):
        for p in range(3):
            for d in range(2):
                send_b(p, da, d).wait_recv()
                go(forward_b(p, da, d))
        if da == 0:
            for p in range(3):
                select(p, 0)
    for p in range(3):
        for db in (3, 1):
            select(p, db)
    for p in range(3):
        relay(p, 0)
    for p in range(3):
        for da in (0, 3, 1, 2):
            for d in range(2):
                forward_b(p, da, d).wait_recv()
        select(p, 2)
    for db in (3, 1, 2):
        for p in range(3):
            relay(p, db)
    for p in range(3):
        for db in range(4):
            for g in range(4):
                cross(p, db, g).wait_recv()
    for copy in weights:
        copy.wait_recv()
    for copy in started:
        copy.wait_send()
    for copy in local:
        copy.wait()


def exchange(tokens, shift, scale, sel, weights):
    any_space = pl.BlockSpec(memory_space=pl.ANY)
    vmem = pl.BlockSpec(memory_space=pltpu.VMEM)
    dma = pltpu.SemaphoreType.DMA
    kv_shape = jax.ShapeDtypeStruct((3, 2, SIDE, SIDE, 8, HALF, PART), jnp.bfloat16)
    return pl.pallas_call(
        exchange_kernel,
        out_shape=[kv_shape] + [jax.ShapeDtypeStruct((2,) + w.shape, w.dtype) for w in weights],
        in_specs=[vmem, vmem, vmem, pl.BlockSpec(memory_space=pltpu.SMEM)] + [any_space] * 6,
        out_specs=[any_space] * 7,
        scratch_shapes=[pltpu.VMEM((SIDE, QB_DEV, HALF, PART), jnp.bfloat16)] * 12
        + [pltpu.VMEM((3, 4, SIDE, 8, HALF, PART), jnp.bfloat16)]
        + [dma((3, 2))] * 4
        + [dma((3, 4, 2))] * 4
        + [dma((3, 4, 4))] * 4
        + [dma((3, 4))]
        + [dma((6,))] * 3,
        compiler_params=pltpu.CompilerParams(
            collective_id=0, has_side_effects=True, vmem_limit_bytes=48 * MIB
        ),
        name="exchange",
    )(tokens, shift, scale, sel, *weights)


ROWS = (1 + KT) * QBLK
OWN = 4 * QBLK
SHARP = HDIM**-0.5 * 1.4426950408889634
WINDOWS = ((0, (0, 1, 2, 3, 4)), (128, (5, 6, 7)))
CHUNK = 512


def block_kernel(
    owner_ref,
    sel_ref,
    count_ref,
    shift_a,
    scale_a,
    gate_a,
    shift_m,
    scale_m,
    gate_m,
    tokens_ref,
    kv_ref,
    wq_h,
    wk_h,
    wv_h,
    wo_h,
    w1_h,
    w2_h,
    out_ref,
    x_ref,
    tok,
    normed,
    queries,
    keys,
    values,
    att,
    wq,
    wk,
    wv,
    wo,
    w1,
    w2,
    sem,
    gsem,
):
    pb = lax.axis_index("pb")
    ha = lax.axis_index("ha")
    me = (pb // 16, (pb // 4) % 4, pb % 4)

    loads = [pltpu.make_async_copy(tokens_ref.at[pl.ds(pl.multiple_of(ha * OWN, OWN), OWN)], tok, sem.at[6])]
    for i, (src, dst) in enumerate(((wq_h, wq), (wk_h, wk), (wv_h, wv), (wo_h, wo), (w1_h, w1), (w2_h, w2))):
        loads.append(pltpu.make_async_copy(src, dst, sem.at[i]))

    def gathers(blk, slot, act):
        for j in range(KT):
            entry = (ha * 4 + blk) * KT + j
            owner = owner_ref[pb, entry]
            first = (sel_ref[pb, owner] & 511) >> 3
            k = jnp.where(first == entry, 0, 1)
            rel = [
                (owner // 16 - me[0]) & 3,
                (owner // 4 - me[1]) & 3,
                (owner - me[2]) & 3,
            ]
            for p in range(3):
                a, b, c = ORDERS[p]
                act(
                    pltpu.make_async_copy(
                        kv_ref.at[p, :, rel[c], rel[b], rel[a] * 2 + k],
                        x_ref.at[slot, 1 + j, :, :, pl.ds(p * PART, PART)],
                        gsem.at[slot, j, p],
                    )
                )

    loads[0].start()
    loads[1].start()
    gathers(0, 0, lambda c: c.start())
    for copy in loads[2:]:
        copy.start()
    loads[0].wait()
    normed[...] = modulate(tok[...].astype(jnp.float32), shift_a[...], scale_a[...]).astype(jnp.bfloat16)
    loads[1].wait()
    for g in range(2):
        queries[g] = jnp.dot(normed[...], wq[g], preferred_element_type=jnp.float32).astype(jnp.bfloat16)
    loads[2].wait()
    loads[3].wait()

    lane = lax.broadcasted_iota(jnp.int32, (QBLK, 256), 1)
    key_pos = lax.broadcasted_iota(jnp.int32, (1, ROWS), 1)

    def one_block(blk, carry):
        slot = lax.rem(blk, 2)

        @pl.when(blk < 3)
        def _():
            gathers(blk + 1, 1 - slot, lambda c: c.start())

        gathers(blk, slot, lambda c: c.wait())
        base = pl.multiple_of(blk * QBLK, QBLK)
        x_ref[slot, 0] = normed[pl.ds(base, QBLK), :].reshape(2, HALF, D)
        x = x_ref[slot].reshape(ROWS, D)
        for g in range(2):
            keys[g] = jnp.dot(x, wk[g], preferred_element_type=jnp.float32).astype(jnp.bfloat16)
            values[g] = jnp.dot(x, wv[g], preferred_element_type=jnp.float32).astype(jnp.bfloat16)
        live = (1 + count_ref[ha * 4 + blk]) * QBLK
        bias = jnp.where(key_pos < live, 0.0, -1e30)

        def one_group(g, carry):
            for lo, heads in WINDOWS:
                q = queries[g, pl.ds(base, QBLK), lo : lo + 256]
                masks = [(lane >= h * HDIM - lo) & (lane < (h + 1) * HDIM - lo) for h in heads]
                stacked = jnp.concatenate([jnp.where(m, q, jnp.zeros_like(q)) for m in masks], 0)
                scores = lax.dot_general(
                    stacked,
                    keys[g, :, lo : lo + 256],
                    (((1,), (1,)), ((), ())),
                    preferred_element_type=jnp.float32,
                )
                scores = scores + bias
                top = jnp.max(scores, -1, keepdims=True)
                weights = jnp.exp2((scores - top) * SHARP)
                totals = jnp.sum(weights, -1, keepdims=True)
                outs = jnp.dot(
                    weights.astype(jnp.bfloat16), values[g, :, lo : lo + 256], preferred_element_type=jnp.float32
                )
                outs = outs / totals
                mixed = jnp.zeros((QBLK, 256), jnp.float32)
                for i, m in enumerate(masks):
                    mixed = jnp.where(m, outs[i * QBLK : (i + 1) * QBLK], mixed)
                mixed = mixed.astype(jnp.bfloat16)
                if lo == 0:
                    att[g, pl.ds(base, QBLK), 0:256] = mixed
                else:
                    first = att[g, pl.ds(base, QBLK), 128:256]
                    att[g, pl.ds(base, QBLK), 128:256] = jnp.where(
                        lane[:, :128] + 128 < 5 * HDIM, first, mixed[:, :128]
                    )
                    att[g, pl.ds(base, QBLK), 256:384] = mixed[:, 128:]
            return carry

        lax.fori_loop(0, 2, one_group, 0)
        return carry

    lax.fori_loop(0, 4, one_block, 0)

    loads[4].wait()
    projected = jnp.dot(att[0], wo[0], preferred_element_type=jnp.float32)
    projected += jnp.dot(att[1], wo[1], preferred_element_type=jnp.float32)
    residual = (tok[...].astype(jnp.float32) + gate_a[...] * projected).astype(jnp.bfloat16)
    tok[...] = residual
    normed[...] = modulate(residual.astype(jnp.float32), shift_m[...], scale_m[...]).astype(jnp.bfloat16)
    loads[5].wait()
    loads[6].wait()
    expanded = jnp.zeros((OWN, D), jnp.float32)
    for g in range(2):
        for lo in range(0, FF // 2, CHUNK):
            hidden = jnp.dot(normed[...], w1[g, :, lo : lo + CHUNK], preferred_element_type=jnp.float32)
            hidden = jax.nn.gelu(hidden, approximate=True).astype(jnp.bfloat16)
            expanded += jnp.dot(hidden, w2[g, lo : lo + CHUNK, :], preferred_element_type=jnp.float32)
    out_ref[...] = (tok[...].astype(jnp.float32) + gate_m[...] * expanded).astype(jnp.bfloat16)


def block(owners, sel, counts, vectors, tokens, kv, weights):
    any_space = pl.BlockSpec(memory_space=pl.ANY)
    vmem = pl.BlockSpec(memory_space=pltpu.VMEM)
    smem = pl.BlockSpec(memory_space=pltpu.SMEM)
    bf16 = jnp.bfloat16
    return pl.pallas_call(
        block_kernel,
        out_shape=jax.ShapeDtypeStruct((OWN, D), bf16),
        in_specs=[smem] * 3 + [vmem] * 6 + [any_space] * 8,
        out_specs=vmem,
        scratch_shapes=[
            pltpu.VMEM((2, 1 + KT, 2, HALF, D), bf16),
            pltpu.VMEM((OWN, D), bf16),
            pltpu.VMEM((OWN, D), bf16),
            pltpu.VMEM((2, OWN, GRP), bf16),
            pltpu.VMEM((2, ROWS, GRP), bf16),
            pltpu.VMEM((2, ROWS, GRP), bf16),
            pltpu.VMEM((2, OWN, GRP), bf16),
        ]
        + [pltpu.VMEM(w.shape, bf16) for w in weights]
        + [pltpu.SemaphoreType.DMA((7,)), pltpu.SemaphoreType.DMA((2, KT, 3))],
        compiler_params=pltpu.CompilerParams(vmem_limit_bytes=56 * MIB),
        name="block",
    )(owners, sel, counts, *vectors, tokens, kv, *weights)


def shards(
    tokens,
    shift_attn,
    scale_attn,
    gate_attn,
    shift_mlp,
    scale_mlp,
    gate_mlp,
    w_query,
    w_key,
    w_value,
    w_out,
    w_fc1,
    w_fc2,
    contact_owner,
    contact_local,
    contact_count,
):
    vectors = [
        v.reshape(1, D) for v in (shift_attn, scale_attn, gate_attn, shift_mlp, scale_mlp, gate_mlp)
    ]
    owners = contact_owner.reshape(N_PB, QB_DEV * KT)
    code = jnp.arange(QB_DEV * KT, dtype=jnp.int32)[None, :] * 8 + contact_local.reshape(N_PB, -1)
    hit = owners[:, :, None] == jnp.arange(N_PB, dtype=jnp.int32)[None, None, :]
    first = jnp.min(jnp.where(hit, code[:, :, None], 511), 1)
    last = jnp.max(jnp.where(hit, code[:, :, None], 0), 1)
    sel = first + (last & 7) * 512
    kv, *weights = exchange(
        tokens, vectors[0], vectors[1], sel, (w_query, w_key, w_value, w_out, w_fc1, w_fc2)
    )
    return block(owners, sel, contact_count, vectors, tokens, kv, weights)


def solution(mesh):
    placed = (
        P("pb", None),
        P(),
        P(),
        P(),
        P(),
        P(),
        P(),
        P(None, "ha"),
        P(None, "ha"),
        P(None, "ha"),
        P("ha", None),
        P(None, "ha"),
        P("ha", None),
        P(),
        P(),
        P("pb"),
    )
    return jax.shard_map(
        shards, mesh=mesh, in_specs=placed, out_specs=P(("pb", "ha"), None), check_vma=False
    )
```

time: 737 us -> 219 us (0.30)
  waiting for transfers between devices: 492 us -> 0 us
  Pallas kernels: 0 us -> 201 us
  other arithmetic: 72 us -> 1.43 us
  local copies, waits for them, and re-layouts: 82.8 us -> 15.8 us
  matrix products: 62.6 us -> 0 us
  between operations: 13.5 us -> 0.29 us
  starting transfers between devices: 12.7 us -> 0 us
    all_to_all x1 -> x0, waiting for transfers between devices: 440 us -> none  [shards(): lax.all_to_all(outgoing, 'pb', split_axis=0, concat_axis=0, tiled=True)]
    pallas_call x0 -> x2, Pallas kernels: none -> 201 us  [the longest x1 154 us: exchange(): pl.pallas_call(exchange_kernel, out_shape=[kv_shape] + [jax.ShapeDtypeStr...]
    dot_general x9 -> x0, matrix products: 62.6 us -> none  [the longest x2 22.7 us: attend(): jnp.einsum('gihd,gjhd->ghij', query_heads, key_heads, preferred_element_t...]
    reduce_scatter x2 -> x0, waiting for transfers between devices: 37.8 us -> none  [the longest x1 24.6 us: shards(): lax.psum_scatter(jnp.dot(attention, w_out, preferred_element_type=jnp.flo...]
    dynamic_slice x8 -> x0, local copies, waits for them, and re-layouts: 36.4 us -> none  [shards(): lax.map(attend_group, (query_groups, kv_groups, mask_groups))]
    select_n x4 -> x0, other arithmetic: 27.9 us -> none  [the longest x2 21.3 us: shards(): outgoing = jnp.take(local_kv, send_block.reshape(-1), axis=0)]
    gather x2 -> x0, local copies, waits for them, and re-layouts: 27.7 us -> none  [the longest x1 15.5 us: shards(): fetched = jnp.take(incoming, entry_index, axis=0)]
    reduce_sum x10 -> x0, other arithmetic: 27.5 us -> none  [the longest x2 18.6 us: attend(): totals = jnp.sum(weights, -1)]
  transfers between devices with their start and end apart: 4 -> 0, of which waited for: 4 -> 0; matrix products, arithmetic and copies ran while one was open for 1% -> 0% of each run, Pallas kernels for 0% -> 0%
where the time goes in v1:
time: 219 us; the launch traced here: 218 us
  Pallas kernels  201 us (92%)
  local copies, waits for them, and re-layouts  15.8 us (7%)
    pallas_call x1, Pallas kernels, exchange(): pl.pallas_call(exchange_kernel, out_shape=[kv_shape] + [jax.ShapeDtypeStr...  154 us
    pallas_call x1, Pallas kernels, block(): pl.pallas_call(block_kernel, out_shape=jax.ShapeDtypeStruct((OWN, D), bf1...  47 us
    unnamed x24, local copies, waits for them, and re-layouts  9.05 us
    reshape x6, local copies, waits for them, and re-layouts, shards(): v.reshape(1, D)  6.47 us

profile of v1, /device:TPU:1, one launch (start us, length us, event | category | flops | bytes accessed | tf_op | source)
XLA Modules:
  0.0 218.2 jit_solution(4679767848780150360)
XLA Ops:
  0.0 0.7 reshape.49.shift_ref.shift_a
  0.7 0.0 copy-start.8
  0.7 0.7 reshape.50.scale_ref.scale_a
  1.4 0.0 copy-start.9
  1.4 1.3 reshape.51.gate_a
  2.7 1.3 reshape.52.shift_m
  3.9 1.3 reshape.53.scale_m
  5.2 1.3 reshape.54.gate_m
  6.5 0.8 copy.20
  7.3 0.1 reshape.47.owner_ref
  7.5 0.0 copy-start.10
  7.5 0.9 copy.21
  8.3 0.1 reshape.48
  8.5 1.4 select_reduce_fusion
  9.9 0.0 copy-start.3
  9.9 1.1 copy-done.3
  11.0 0.0 copy-start.4
  11.0 1.1 copy-done.4
  12.1 0.0 copy-start.5
  12.1 1.1 copy-done.5
  13.1 0.0 copy-start.6
  13.1 1.1 copy-done.6
  14.2 0.0 copy-start.7
  14.2 153.6 %exchange.1 = (bf16[3,2,4,4,8,64,256]{6,5,4,3,2,1,0:T(8,128)(2,1)}, bf16[2,768,384]{2,1,0:T(8,128)(2,1)S(1)}, bf16[2,768,384]{2,1,0:T(8,128)(2,1)S(1)}, bf16[2,7...) custom-call(bf16[1024,768]{1,0:T(8,128)(2,1)} %tokens_ref.3, ...), custom_call_target="tpu_custom_call" | custom-call | tf_op jit(solution)/shard_map/exchange/pallas_call | solution.py:232
  167.8 0.0 copy-done.8
  167.8 0.0 copy-done.9
  167.9 0.0 copy-done.10
  167.9 0.0 copy-done.7
  167.9 0.0 copy-start
  167.9 1.0 copy-done
  168.9 0.0 copy-start.1
  168.9 1.0 copy-done.1
  170.0 0.0 copy-start.2
  170.0 1.0 copy-done.2
  171.0 47.0 %block.1 = bf16[512,768]{1,0:T(8,128)(2,1)} custom-call(s32[64,64]{1,0:T(8,128)} %copy-done.10, s32[64,64]{1,0:T(8,128)} %copy-done.7, s32[8]{0:T(128)} %count_ref.1, f32[1,768]{1,0:T(1,128)} %copy-done.8, f32[1,768]{1,0:T(1,128)} %copy-done.9, f32[1,768]{1,0:T(1,128)} %reshape.51.gate_a, f32[1,768]{1,0:T(1,128)} %reshape.52.shift_m, ...), custom_call_target="tpu_custom_call" | custom-call | tf_op jit(solution)/shard_map/block/pallas_call | solution.py:415
  (3 shorter events, 0.0 us)
Async XLA Ops:
  0.7 167.1 %copy-start.8 = (f32[1,768]{1,0:T(1,128)}, f32[1,768]{1,0:T(1,128)S(1)}, u32[]{:S(2)}) copy-start(f32[1,768]{1,0:T(1,128)S(1)} %reshape.49.shift_ref.shift_a) | copy-start | bytes 9220
  1.4 166.5 %copy-start.9 = (f32[1,768]{1,0:T(1,128)}, f32[1,768]{1,0:T(1,128)S(1)}, u32[]{:S(2)}) copy-start(f32[1,768]{1,0:T(1,128)S(1)} %reshape.50.scale_ref.scale_a) | copy-start | bytes 9220
  7.5 160.4 %copy-start.10 = (s32[64,64]{1,0:T(8,128)}, s32[64,64]{1,0:T(8,128)S(1)}, u32[]{:S(2)}) copy-start(s32[64,64]{1,0:T(8,128)S(1)} %reshape.47.owner_ref) | copy-start | bytes 49156
  9.9 1.1 copy-start.3
  11.0 1.1 copy-start.4
  12.1 1.1 copy-start.5
  13.1 1.1 copy-start.6
  14.2 153.7 %copy-start.7 = (s32[64,64]{1,0:T(8,128)}, s32[64,64]{1,0:T(8,128)S(1)}, u32[]{:S(2)}) copy-start(s32[64,64]{1,0:T(8,128)S(1)} %multiply_add_fusion.sel_ref) | copy-start | bytes 49156
  167.9 1.0 copy-start
  168.9 1.1 copy-start.1
  170.0 1.0 copy-start.2

commit v2 on v1

--- a/solution.py
+++ b/solution.py
@@ -33,15 +33,15 @@
     return center * lax.rsqrt(spread + epsilon) * (1.0 + scale) + shift
 
 
-def exchange_kernel(
-    tokens_ref, shift_ref, scale_ref, sel_ref, *refs
-):
+def exchange_kernel(tokens_ref, shift_ref, scale_ref, owner_ref, block_ref, *refs):
     w_in = refs[0:6]
     kv_ref = refs[6]
-    w_out = refs[7:13]
-    rows = [refs[13 + 4 * p : 17 + 4 * p] for p in range(3)]
-    picked = refs[25]
-    (a_s, a_r, af_s, af_r, b_s, b_r, bf_s, bf_r, c_s, c_r, x_s, x_r, l_s, w_s, w_r, wl_s) = refs[26:]
+    sel_out = refs[7]
+    w_out = refs[8:14]
+    rows = [refs[14 + 4 * p : 18 + 4 * p] for p in range(3)]
+    picked = refs[26]
+    tok, shift, scale, owners, blocks, table, sel_ref = refs[27:34]
+    (a_s, a_r, af_s, af_r, b_s, b_r, bf_s, bf_r, c_s, c_r, x_s, x_r, l_s, w_s, w_r, t_s, v_s) = refs[34:]
 
     pb = lax.axis_index("pb")
     ha = lax.axis_index("ha")
@@ -60,19 +60,34 @@
             src_ref=src, dst_ref=dst, send_sem=ssem, recv_sem=rsem, device_id=dev, device_id_type=MESH
         )
 
-    def norm_tile(t, carry):
-        x = tokens_ref[pl.ds(pl.multiple_of(t * QBLK + ha * HALF, HALF), HALF), :].astype(jnp.float32)
-        n = modulate(x, shift_ref[...], scale_ref[...]).astype(jnp.bfloat16)
-        for p in range(3):
-            rows[p][0][0, t] = n[:, p * PART : (p + 1) * PART]
-        return carry
+    half_rows = [
+        pltpu.make_async_copy(
+            tokens_ref.at[pl.ds(pl.multiple_of(t * QBLK + ha * HALF, HALF), HALF)], tok.at[t], t_s.at[t]
+        )
+        for t in range(QB_DEV)
+    ]
+    small = [
+        pltpu.make_async_copy(src, dst, v_s.at[i])
+        for i, (src, dst) in enumerate(
+            ((shift_ref, shift), (scale_ref, scale), (owner_ref, owners), (block_ref, blocks))
+        )
+    ]
+    for copy in small + half_rows:
+        copy.start()
 
     barrier = pltpu.get_barrier_semaphore()
     for axis in range(3):
         for off in (1, 2, 3):
             pl.semaphore_signal(barrier, 1, device_id=chip(axis, off), device_id_type=MESH)
     pl.semaphore_signal(barrier, 1, device_id=other, device_id_type=MESH)
-    lax.fori_loop(0, QB_DEV, norm_tile, 0)
+    small[0].wait()
+    small[1].wait()
+    for t in range(QB_DEV):
+        half_rows[t].wait()
+        n = modulate(tok[t].astype(jnp.float32), shift[...].reshape(1, D), scale[...].reshape(1, D))
+        n = n.astype(jnp.bfloat16)
+        for p in range(3):
+            rows[p][0][0, t] = n[:, p * PART : (p + 1) * PART]
     pl.semaphore_wait(barrier, 10)
 
     started = []
@@ -149,7 +164,7 @@
             def pick(j, carry):
                 da, k = j // 2, j % 2
                 owner = moved(moved(pb, b, db), a, da)
-                code = sel_ref[dest, owner]
+                code = sel_ref[owner, dest * QB_DEV]
                 number = jnp.where(k == 0, code & 7, (code >> 9) & 7)
                 picked[p, g, db, j] = rows[p][db][da, number]
                 return carry
@@ -172,13 +187,34 @@
     for p in range(3):
         for d in range(2):
             go(send_b(p, 0, d))
-    weights = [remote(w_in[i], w_out[i].at[ha], w_s.at[i], w_r.at[i], other) for i in range(6)]
-    kept = [pltpu.make_async_copy(w_in[i], w_out[i].at[ha], wl_s.at[i]) for i in range(6)]
+    weights = [remote(w_in[i], w_out[i], w_s.at[i], w_r.at[i], other) for i in range(6)]
     for copy in weights:
         go(copy)
-    for copy in kept:
-        local.append(copy)
-        copy.start()
+
+    small[2].wait()
+    small[3].wait()
+    lane = lax.broadcasted_iota(jnp.int32, (KT, N_PB * QB_DEV), 1)
+    order = (lane & 7) * KT + lax.broadcasted_iota(jnp.int32, (KT, N_PB * QB_DEV), 0)
+    code = order * 8 + blocks[...]
+    size = N_PB * QB_DEV
+
+    def tabulate(o, carry):
+        hit = owners[...] == o
+        first = jnp.where(hit, code, 511)
+        last = jnp.where(hit, code, 0)
+        for step in (1, 2, 4):
+            first = jnp.minimum(first, pltpu.roll(first, size - step, 1))
+            last = jnp.maximum(last, pltpu.roll(last, size - step, 1))
+        first = jnp.min(first, 0, keepdims=True)
+        last = jnp.max(last, 0, keepdims=True)
+        table[pl.ds(o, 1), :] = first + (last & 7) * 512
+        return carry
+
+    lax.fori_loop(0, N_PB, tabulate, 0)
+    to_scalars = pltpu.make_async_copy(table, sel_ref, v_s.at[4])
+    to_scalars.start()
+    local.append(pltpu.make_async_copy(table, sel_out, v_s.at[5]))
+    local[-1].start()
     for p in range(3):
         for d in range(2):
             send_a(p, d).wait_recv()
@@ -197,6 +233,7 @@
                 send_b(p, da, d).wait_recv()
                 go(forward_b(p, da, d))
         if da == 0:
+            to_scalars.wait()
             for p in range(3):
                 select(p, 0)
     for p in range(3):
@@ -224,28 +261,37 @@
         copy.wait()
 
 
-def exchange(tokens, shift, scale, sel, weights):
-    any_space = pl.BlockSpec(memory_space=pl.ANY)
-    vmem = pl.BlockSpec(memory_space=pltpu.VMEM)
+HBM = pl.BlockSpec(memory_space=pltpu.HBM)
+
+
+def exchange(tokens, shift, scale, owners, blocks, weights):
     dma = pltpu.SemaphoreType.DMA
-    kv_shape = jax.ShapeDtypeStruct((3, 2, SIDE, SIDE, 8, HALF, PART), jnp.bfloat16)
+    bf16 = jnp.bfloat16
+    kv_shape = jax.ShapeDtypeStruct((3, 2, SIDE, SIDE, 8, HALF, PART), bf16)
+    table = (N_PB, N_PB * QB_DEV)
     return pl.pallas_call(
         exchange_kernel,
-        out_shape=[kv_shape] + [jax.ShapeDtypeStruct((2,) + w.shape, w.dtype) for w in weights],
-        in_specs=[vmem, vmem, vmem, pl.BlockSpec(memory_space=pltpu.SMEM)] + [any_space] * 6,
-        out_specs=[any_space] * 7,
-        scratch_shapes=[pltpu.VMEM((SIDE, QB_DEV, HALF, PART), jnp.bfloat16)] * 12
-        + [pltpu.VMEM((3, 4, SIDE, 8, HALF, PART), jnp.bfloat16)]
+        out_shape=[kv_shape, jax.ShapeDtypeStruct(table, jnp.int32)]
+        + [jax.ShapeDtypeStruct(w.shape, w.dtype) for w in weights],
+        in_specs=[HBM] * 11,
+        out_specs=[HBM] * 8,
+        scratch_shapes=[pltpu.VMEM((SIDE, QB_DEV, HALF, PART), bf16)] * 12
+        + [pltpu.VMEM((3, 4, SIDE, 8, HALF, PART), bf16)]
+        + [pltpu.VMEM((QB_DEV, HALF, D), bf16)]
+        + [pltpu.VMEM((D,), jnp.float32)] * 2
+        + [pltpu.VMEM((KT, N_PB * QB_DEV), jnp.int32)] * 2
+        + [pltpu.VMEM(table, jnp.int32), pltpu.SMEM(table, jnp.int32)]
         + [dma((3, 2))] * 4
         + [dma((3, 4, 2))] * 4
         + [dma((3, 4, 4))] * 4
         + [dma((3, 4))]
-        + [dma((6,))] * 3,
+        + [dma((6,))] * 2
+        + [dma((QB_DEV,)), dma((6,))],
         compiler_params=pltpu.CompilerParams(
-            collective_id=0, has_side_effects=True, vmem_limit_bytes=48 * MIB
+            collective_id=0, has_side_effects=True, vmem_limit_bytes=62 * MIB
         ),
         name="exchange",
-    )(tokens, shift, scale, sel, *weights)
+    )(tokens, shift, scale, owners, blocks, *weights)
 
 
 ROWS = (1 + KT) * QBLK
@@ -256,53 +302,63 @@
 
 
 def block_kernel(
-    owner_ref,
-    sel_ref,
     count_ref,
-    shift_a,
-    scale_a,
-    gate_a,
-    shift_m,
-    scale_m,
-    gate_m,
-    tokens_ref,
-    kv_ref,
-    wq_h,
-    wk_h,
-    wv_h,
-    wo_h,
-    w1_h,
-    w2_h,
-    out_ref,
-    x_ref,
-    tok,
-    normed,
-    queries,
-    keys,
-    values,
-    att,
-    wq,
-    wk,
-    wv,
-    wo,
-    w1,
-    w2,
-    sem,
-    gsem,
+    owner_h,
+    sel_h,
+    *refs,
 ):
+    vectors_h = refs[0:6]
+    tokens_ref, kv_ref = refs[6:8]
+    own_h, other_h = refs[8:14], refs[14:20]
+    out_ref, owner_ref, sel_ref = refs[20:23]
+    vectors = refs[23:29]
+    x_ref, tok, normed, queries, keys, values, att = refs[29:36]
+    held = refs[36:42]
+    wq, wk, wv, wo, w1, w2 = held
+    sem, vsem, gsem = refs[42:]
+    shift_a, scale_a, gate_a, shift_m, scale_m, gate_m = vectors
+
+    def row(vector):
+        return vector[...].reshape(1, D)
+
     pb = lax.axis_index("pb")
     ha = lax.axis_index("ha")
     me = (pb // 16, (pb // 4) % 4, pb % 4)
 
-    loads = [pltpu.make_async_copy(tokens_ref.at[pl.ds(pl.multiple_of(ha * OWN, OWN), OWN)], tok, sem.at[6])]
-    for i, (src, dst) in enumerate(((wq_h, wq), (wk_h, wk), (wv_h, wv), (wo_h, wo), (w1_h, w1), (w2_h, w2))):
-        loads.append(pltpu.make_async_copy(src, dst, sem.at[i]))
+    base_lane = pl.multiple_of((pb // 16) * 128, 128)
+    my_lane = (pb % 16) * QB_DEV
+    tables = [
+        pltpu.make_async_copy(owner_h.at[:, pl.ds(base_lane, 128)], owner_ref, vsem.at[6]),
+        pltpu.make_async_copy(sel_h.at[:, pl.ds(base_lane, 128)], sel_ref, vsem.at[7]),
+    ]
+    small = [pltpu.make_async_copy(vectors_h[i], vectors[i], vsem.at[i]) for i in range(6)]
+    tokens_in = pltpu.make_async_copy(
+        tokens_ref.at[pl.ds(pl.multiple_of(ha * OWN, OWN), OWN)], tok, sem.at[12]
+    )
+    loads = []
+    for i in range(6):
+        loads.append(
+            (
+                pltpu.make_async_copy(own_h[i], held[i].at[ha], sem.at[i]),
+                pltpu.make_async_copy(other_h[i], held[i].at[1 - ha], sem.at[6 + i]),
+            )
+        )
+
+    def begin(*numbers):
+        for i in numbers:
+            loads[i][0].start()
+            loads[i][1].start()
+
+    def ready(*numbers):
+        for i in numbers:
+            loads[i][0].wait()
+            loads[i][1].wait()
 
     def gathers(blk, slot, act):
         for j in range(KT):
             entry = (ha * 4 + blk) * KT + j
-            owner = owner_ref[pb, entry]
-            first = (sel_ref[pb, owner] & 511) >> 3
+            owner = owner_ref[j, my_lane + ha * 4 + blk]
+            first = (sel_ref[owner, my_lane] & 511) >> 3
             k = jnp.where(first == entry, 0, 1)
             rel = [
                 (owner // 16 - me[0]) & 3,
@@ -319,18 +375,22 @@
                     )
                 )
 
-    loads[0].start()
-    loads[1].start()
+    for copy in tables + small:
+        copy.start()
+    tokens_in.start()
+    begin(0, 1, 2)
+    for copy in tables:
+        copy.wait()
     gathers(0, 0, lambda c: c.start())
-    for copy in loads[2:]:
-        copy.start()
-    loads[0].wait()
-    normed[...] = modulate(tok[...].astype(jnp.float32), shift_a[...], scale_a[...]).astype(jnp.bfloat16)
-    loads[1].wait()
+    begin(3, 4, 5)
+    for copy in small:
+        copy.wait()
+    tokens_in.wait()
+    normed[...] = modulate(tok[...].astype(jnp.float32), row(shift_a), row(scale_a)).astype(jnp.bfloat16)
+    ready(0)
     for g in range(2):
         queries[g] = jnp.dot(normed[...], wq[g], preferred_element_type=jnp.float32).astype(jnp.bfloat16)
-    loads[2].wait()
-    loads[3].wait()
+    ready(1, 2)
 
     lane = lax.broadcasted_iota(jnp.int32, (QBLK, 256), 1)
     key_pos = lax.broadcasted_iota(jnp.int32, (1, ROWS), 1)
@@ -390,34 +450,32 @@
 
     lax.fori_loop(0, 4, one_block, 0)
 
-    loads[4].wait()
+    ready(3)
     projected = jnp.dot(att[0], wo[0], preferred_element_type=jnp.float32)
     projected += jnp.dot(att[1], wo[1], preferred_element_type=jnp.float32)
-    residual = (tok[...].astype(jnp.float32) + gate_a[...] * projected).astype(jnp.bfloat16)
+    residual = (tok[...].astype(jnp.float32) + row(gate_a) * projected).astype(jnp.bfloat16)
     tok[...] = residual
-    normed[...] = modulate(residual.astype(jnp.float32), shift_m[...], scale_m[...]).astype(jnp.bfloat16)
-    loads[5].wait()
-    loads[6].wait()
+    normed[...] = modulate(residual.astype(jnp.float32), row(shift_m), row(scale_m)).astype(jnp.bfloat16)
+    ready(4, 5)
     expanded = jnp.zeros((OWN, D), jnp.float32)
     for g in range(2):
         for lo in range(0, FF // 2, CHUNK):
             hidden = jnp.dot(normed[...], w1[g, :, lo : lo + CHUNK], preferred_element_type=jnp.float32)
             hidden = jax.nn.gelu(hidden, approximate=True).astype(jnp.bfloat16)
             expanded += jnp.dot(hidden, w2[g, lo : lo + CHUNK, :], preferred_element_type=jnp.float32)
-    out_ref[...] = (tok[...].astype(jnp.float32) + gate_m[...] * expanded).astype(jnp.bfloat16)
-
-
-def block(owners, sel, counts, vectors, tokens, kv, weights):
-    any_space = pl.BlockSpec(memory_space=pl.ANY)
-    vmem = pl.BlockSpec(memory_space=pltpu.VMEM)
-    smem = pl.BlockSpec(memory_space=pltpu.SMEM)
+    out_ref[...] = (tok[...].astype(jnp.float32) + row(gate_m) * expanded).astype(jnp.bfloat16)
+
+
+def block(counts, owners, sel, vectors, tokens, kv, own, other):
     bf16 = jnp.bfloat16
     return pl.pallas_call(
         block_kernel,
         out_shape=jax.ShapeDtypeStruct((OWN, D), bf16),
-        in_specs=[smem] * 3 + [vmem] * 6 + [any_space] * 8,
-        out_specs=vmem,
-        scratch_shapes=[
+        in_specs=[pl.BlockSpec(memory_space=pltpu.SMEM)] + [HBM] * 22,
+        out_specs=pl.BlockSpec(memory_space=pltpu.VMEM),
+        scratch_shapes=[pltpu.SMEM((KT, 128), jnp.int32), pltpu.SMEM((N_PB, 128), jnp.int32)]
+        + [pltpu.VMEM((D,), jnp.float32)] * 6
+        + [
             pltpu.VMEM((2, 1 + KT, 2, HALF, D), bf16),
             pltpu.VMEM((OWN, D), bf16),
             pltpu.VMEM((OWN, D), bf16),
@@ -426,11 +484,15 @@
             pltpu.VMEM((2, ROWS, GRP), bf16),
             pltpu.VMEM((2, OWN, GRP), bf16),
         ]
-        + [pltpu.VMEM(w.shape, bf16) for w in weights]
-        + [pltpu.SemaphoreType.DMA((7,)), pltpu.SemaphoreType.DMA((2, KT, 3))],
-        compiler_params=pltpu.CompilerParams(vmem_limit_bytes=56 * MIB),
+        + [pltpu.VMEM((2,) + w.shape, bf16) for w in own]
+        + [
+            pltpu.SemaphoreType.DMA((13,)),
+            pltpu.SemaphoreType.DMA((8,)),
+            pltpu.SemaphoreType.DMA((2, KT, 3)),
+        ],
+        compiler_params=pltpu.CompilerParams(vmem_limit_bytes=62 * MIB),
         name="block",
-    )(owners, sel, counts, *vectors, tokens, kv, *weights)
+    )(counts, owners, sel, *vectors, tokens, kv, *own, *other)
 
 
 def shards(
@@ -451,19 +513,11 @@
     contact_local,
     contact_count,
 ):
-    vectors = [
-        v.reshape(1, D) for v in (shift_attn, scale_attn, gate_attn, shift_mlp, scale_mlp, gate_mlp)
-    ]
-    owners = contact_owner.reshape(N_PB, QB_DEV * KT)
-    code = jnp.arange(QB_DEV * KT, dtype=jnp.int32)[None, :] * 8 + contact_local.reshape(N_PB, -1)
-    hit = owners[:, :, None] == jnp.arange(N_PB, dtype=jnp.int32)[None, None, :]
-    first = jnp.min(jnp.where(hit, code[:, :, None], 511), 1)
-    last = jnp.max(jnp.where(hit, code[:, :, None], 0), 1)
-    sel = first + (last & 7) * 512
-    kv, *weights = exchange(
-        tokens, vectors[0], vectors[1], sel, (w_query, w_key, w_value, w_out, w_fc1, w_fc2)
-    )
-    return block(owners, sel, contact_count, vectors, tokens, kv, weights)
+    vectors = (shift_attn, scale_attn, gate_attn, shift_mlp, scale_mlp, gate_mlp)
+    own = (w_query, w_key, w_value, w_out, w_fc1, w_fc2)
+    owners, blocks = contact_owner.T, contact_local.T
+    kv, sel, *other = exchange(tokens, shift_attn, scale_attn, owners, blocks, own)
+    return block(contact_count, owners, sel, vectors, tokens, kv, own, other)
 
 
 def solution(mesh):

time: 219 us -> 158 us (0.72)
  Pallas kernels: 201 us -> 158 us
  local copies, waits for them, and re-layouts: 15.8 us -> 0 us
    pallas_call x1, Pallas kernels: 154 us -> 111 us  [exchange(): pl.pallas_call(exchange_kernel, out_shape=[kv_shape, jax.ShapeDtypeStruct...]
    unnamed x24 -> x0, local copies, waits for them, and re-layouts: 9.05 us -> none
    reshape x8 -> x0, local copies, waits for them, and re-layouts: 6.73 us -> none  [the longest x6 6.47 us: shards(): v.reshape(1, D)]
where the time goes in v2:
time: 158 us
  Pallas kernels  158 us (100%)
    pallas_call x1, Pallas kernels, exchange(): pl.pallas_call(exchange_kernel, out_shape=[kv_shape, jax.ShapeDtypeStruct...  111 us
    pallas_call x1, Pallas kernels, block(): pl.pallas_call(block_kernel, out_shape=jax.ShapeDtypeStruct((OWN, D), bf1...  47.4 us

profile of v2, /device:TPU:1, one launch (start us, length us, event | category | flops | bytes accessed | tf_op | source)
XLA Modules:
  0.0 158.0 jit_solution(6394358834681361115)
XLA Ops:
  0.0 110.5 %exchange.1 = (bf16[3,2,4,4,8,64,256]{6,5,4,3,2,1,0:T(8,128)(2,1)}, s32[64,512]{1,0:T(8,128)}, bf16[768,384]{1,0:T(8,128)(2,1)}, bf16[768,384]{1,0:T(8,128)(2,1)...) custom-call(bf16[1024,768]{1,0:T(8,128)(2,1)} %refs_6_.1, ...), custom_call_target="tpu_custom_call" | custom-call | tf_op jit(solution)/shard_map/exchange/pallas_call | solution.py:272
  110.5 47.4 %block.1 = bf16[512,768]{1,0:T(8,128)(2,1)} custom-call(s32[8]{0:T(128)} %count_ref.1, s32[8,512]{1,0:T(8,128)} %bitcast.3, s32[64,512]{1,0:T(8,128)} %get-tuple-element.13.sel_h, f32[768]{0:T(1024)} %refs_0_.3, f32[768]{0:T(1024)} %refs_1_.3, f32[768]{0:T(1024)} %refs_2_.3, f32[768]{0:T(1024)} %refs_3_.3, f32[768]{0:T(1024)} %refs_4_.3, f32[768]{0:T(1024)} %refs_5_.3, ...), custom_call_target="tpu_custom_call" | custom-call | tf_op jit(solution)/shard_map/block/pallas_call | solution.py:471

commit v3 on v2

v3 whole, which is shorter than its diff:
```python
import jax
import jax.numpy as jnp
from jax import lax
from jax.experimental import pallas as pl
from jax.experimental.pallas import tpu as pltpu
from jax.sharding import PartitionSpec as P

D = 768
HEADS = 16
HDIM = 48
FF = 3072
QBLK = 128
KT = 8
QB_DEV = 8
N_PB = 64
SIDE = 4
HALF = QBLK // 2
PART = D // 3
GRP = D // 2
MIB = 2**20
MESH = pl.DeviceIdType.MESH

ORDERS = ((2, 1, 0), (1, 0, 2), (0, 2, 1))
STRIDES = (16, 4, 1)
OFFS = (0, 1, 3, 2)

epsilon = 1e-06


def modulate(stream, shift, scale):
    center = stream - jnp.mean(stream, -1, keepdims=True)
    spread = jnp.mean(center * center, -1, keepdims=True)
    return center * lax.rsqrt(spread + epsilon) * (1.0 + scale) + shift


ROWS = (1 + KT) * QBLK
OWN = 4 * QBLK
SHARP = HDIM**-0.5 * 1.4426950408889634
WINDOWS = ((0, (0, 1, 2, 3, 4), 255), (128, (5, 6, 7), 0))
CHUNK = 512
DEAD = -1e30


def with_lane(value, lane, fill):
    at = lax.broadcasted_iota(jnp.int32, (value.shape[0], 128), 1)
    left, right = value[:, :128], value[:, 128:]
    if lane == 0:
        left = jnp.where(at == 0, fill, left)
    else:
        right = jnp.where(at == 127, fill, right)
    return jnp.concatenate([left, right], 1)


def exchange_kernel(tokens_ref, shift_ref, scale_ref, owner_ref, block_ref, *refs):
    w_in = refs[0:6]
    kv_ref, place_out, q_out, mine_out = refs[6:10]
    w_out = refs[10:15]
    rows = [refs[15 + 4 * p : 19 + 4 * p] for p in range(3)]
    picked = refs[27]
    tok, shift, scale, owners, blocks, table, sel_ref, owner_s, places = refs[28:37]
    own, qkv_w, queries, mine = refs[37:41]
    (a_s, a_r, af_s, af_r, b_s, b_r, bf_s, bf_r, c_s, c_r, x_s, x_r, l_s, w_s, w_r, t_s, v_s) = refs[41:]

    pb = lax.axis_index("pb")
    ha = lax.axis_index("ha")
    me = (pb // 16, (pb // 4) % 4, pb % 4)

    def moved(base, axis, off):
        return base + (lax.rem(me[axis] + off, SIDE) - me[axis]) * STRIDES[axis]

    def chip(axis, off):
        return {"pb": moved(pb, axis, off), "ha": ha}

    other = {"pb": pb, "ha": 1 - ha}

    def remote(src, dst, ssem, rsem, dev):
        return pltpu.make_async_remote_copy(
            src_ref=src, dst_ref=dst, send_sem=ssem, recv_sem=rsem, device_id=dev, device_id_type=MESH
        )

    half_rows = [
        pltpu.make_async_copy(
            tokens_ref.at[pl.ds(pl.multiple_of(t * QBLK + ha * HALF, HALF), HALF)], tok.at[t], t_s.at[t]
        )
        for t in range(QB_DEV)
    ]
    small = [
        pltpu.make_async_copy(src, dst, v_s.at[i])
        for i, (src, dst) in enumerate(
            (
                (shift_ref, shift),
                (scale_ref, scale),
                (owner_ref, owners),
                (block_ref, blocks),
                (owner_ref, owner_s),
                (tokens_ref.at[pl.ds(pl.multiple_of(ha * OWN, OWN), OWN)], own),
                (w_in[0], qkv_w.at[0, ha]),
                (w_in[1], qkv_w.at[1, ha]),
                (w_in[2], qkv_w.at[2, ha]),
            )
        )
    ]
    for copy in small[:2] + half_rows + small[2:]:
        copy.start()

    barrier = pltpu.get_barrier_semaphore()
    for axis in range(3):
        for off in (1, 2, 3):
            pl.semaphore_signal(barrier, 1, device_id=chip(axis, off), device_id_type=MESH)
    pl.semaphore_signal(barrier, 1, device_id=other, device_id_type=MESH)
    small[0].wait()
    small[1].wait()
    for t in range(QB_DEV):
        half_rows[t].wait()
        n = modulate(tok[t].astype(jnp.float32), shift[...].reshape(1, D), scale[...].reshape(1, D))
        n = n.astype(jnp.bfloat16)
        for p in range(3):
            rows[p][0][0, t] = n[:, p * PART : (p + 1) * PART]
    pl.semaphore_wait(barrier, 10)

    started = []

    def go(copy):
        copy.start()
        started.append(copy)

    local = []

    def send_a(p, d):
        a = ORDERS[p][0]
        return remote(
            rows[p][0].at[0], rows[p][0].at[3 if d == 0 else 1], a_s.at[p, d], a_r.at[p, d], chip(a, 1 if d == 0 else 3)
        )

    def forward_a(p, d):
        a = ORDERS[p][0]
        part = pl.ds(4 * d, 4)
        return remote(
            rows[p][0].at[3 if d == 0 else 1, part],
            rows[p][0].at[2, part],
            af_s.at[p, d],
            af_r.at[p, d],
            chip(a, 1 if d == 0 else 3),
        )

    def send_b(p, da, d):
        b = ORDERS[p][1]
        return remote(
            rows[p][0].at[da],
            rows[p][3 if d == 0 else 1].at[da],
            b_s.at[p, da, d],
            b_r.at[p, da, d],
            chip(b, 1 if d == 0 else 3),
        )

    def forward_b(p, da, d):
        b = ORDERS[p][1]
        part = pl.ds(4 * d, 4)
        return remote(
            rows[p][3 if d == 0 else 1].at[da, part],
            rows[p][2].at[da, part],
            bf_s.at[p, da, d],
            bf_r.at[p, da, d],
            chip(b, 1 if d == 0 else 3),
        )

    def send_c(p, db, g):
        c = ORDERS[p][2]
        off = OFFS[g]
        return remote(
            picked.at[p, g, db],
            kv_ref.at[p, 0, SIDE - off, db],
            c_s.at[p, db, g],
            c_r.at[p, db, g],
            chip(c, off),
        )

    def cross(p, db, g):
        src = picked.at[p, 0, db] if g == 0 else kv_ref.at[p, 0, SIDE - OFFS[g], db]
        return remote(
            src, kv_ref.at[p, 1, (SIDE - OFFS[g]) % SIDE, db], x_s.at[p, db, g], x_r.at[p, db, g], other
        )

    def keep(p, db):
        return pltpu.make_async_copy(picked.at[p, 0, db], kv_ref.at[p, 0, 0, db], l_s.at[p, db])

    def select(p, db):
        a, b, c = ORDERS[p]
        for g in range(4):
            dest = moved(pb, c, OFFS[g])

            def pick(j, carry):
                da, k = j // 2, j % 2
                owner = moved(moved(pb, b, db), a, da)
                code = sel_ref[owner, dest * QB_DEV]
                number = jnp.where(k == 0, code & 7, (code >> 9) & 7)
                picked[p, g, db, j] = rows[p][db][da, number]
                return carry

            lax.fori_loop(0, 8, pick, 0)
        for g in (3, 1, 2):
            go(send_c(p, db, g))
        local.append(keep(p, db))
        local[-1].start()
        go(cross(p, db, 0))

    def relay(p, db):
        for g in (1, 2, 3):
            send_c(p, db, g).wait_recv()
            go(cross(p, db, g))

    for p in range(3):
        for d in range(2):
            go(send_a(p, d))
    for p in range(3):
        for d in range(2):
            go(send_b(p, 0, d))
    weights = [
        remote(w_in[i], qkv_w.at[i, ha] if i < 3 else w_out[i - 1], w_s.at[i], w_r.at[i], other)
        for i in range(6)
    ]
    for copy in weights:
        go(copy)

    small[2].wait()
    small[3].wait()
    lane = lax.broadcasted_iota(jnp.int32, (KT, N_PB * QB_DEV), 1)
    order = (lane & 7) * KT + lax.broadcasted_iota(jnp.int32, (KT, N_PB * QB_DEV), 0)
    code = order * 8 + blocks[...]
    size = N_PB * QB_DEV

    def tabulate(o, carry):
        hit = owners[...] == o
        first = jnp.where(hit, code, 511)
        last = jnp.where(hit, code, 0)
        for step in (1, 2, 4):
            first = jnp.minimum(first, pltpu.roll(first, size - step, 1))
            last = jnp.maximum(last, pltpu.roll(last, size - step, 1))
        first = jnp.min(first, 0, keepdims=True)
        last = jnp.max(last, 0, keepdims=True)
        table[pl.ds(o, 1), :] = first + (last & 7) * 512
        return carry

    lax.fori_loop(0, N_PB, tabulate, 0)
    to_scalars = pltpu.make_async_copy(table, sel_ref, v_s.at[9])
    to_scalars.start()

    def keep_local(src, dst, number):
        local.append(pltpu.make_async_copy(src, dst, v_s.at[number]))
        local[-1].start()

    def place_entry(e, carry):
        i, j = e // KT, e % KT
        owner = owner_s[j, pb * QB_DEV + ha * 4 + i]
        first = (sel_ref[owner, pb * QB_DEV] & 511) >> 3
        k = jnp.where(first == ha * 4 * KT + e, 0, 1)
        rel = ((owner // 16 - me[0]) & 3, (owner // 4 - me[1]) & 3, (owner - me[2]) & 3)
        for p in range(3):
            a, b, c = ORDERS[p]
            places[p, e] = ((rel[c] * 4 + rel[b]) * 4 + rel[a]) * 2 + k
        return carry

    def own_blocks():
        small[5].wait()
        normed = modulate(own[...].astype(jnp.float32), shift[...].reshape(1, D), scale[...].reshape(1, D))
        own[...] = normed.astype(jnp.bfloat16)
        for i in range(3):
            small[6 + i].wait()
            remote(w_in[i], qkv_w.at[i, 1 - ha], w_s.at[i], w_r.at[i], other).wait_recv()
        keep_local(qkv_w.at[1, 1 - ha], w_out[0], 10)
        keep_local(qkv_w.at[2, 1 - ha], w_out[1], 11)

        def one_group(g, carry):
            def product(i):
                return jnp.dot(own[...], qkv_w[i, g], preferred_element_type=jnp.float32)

            queries[g] = (product(0) * SHARP).astype(jnp.bfloat16)
            for i in range(2):
                result = product(1 + i).astype(jnp.bfloat16)
                fill = jnp.full((QBLK, 128), float(i), jnp.bfloat16)
                for w, (lo, _, spare) in enumerate(WINDOWS):
                    for blk in range(4):
                        mine[blk, g, w, i] = with_lane(
                            result[blk * QBLK : (blk + 1) * QBLK, lo : lo + 256], spare, fill
                        )
            return carry

        lax.fori_loop(0, 2, one_group, 0)
        keep_local(queries, q_out, 12)
        keep_local(mine, mine_out, 13)
        lax.fori_loop(0, 4 * KT, place_entry, 0)
        keep_local(places, place_out, 14)

    for p in range(3):
        for d in range(2):
            send_a(p, d).wait_recv()
            go(forward_a(p, d))
        for d in range(2):
            for da in (3, 1):
                go(send_b(p, da, d))
    for p in range(3):
        for d in range(2):
            forward_a(p, d).wait_recv()
        for d in range(2):
            go(send_b(p, 2, d))
    to_scalars.wait()
    small[4].wait()
    for p in range(3):
        select(p, 0)
    own_blocks()
    for da in (0, 3, 1, 2):
        for p in range(3):
            for d in range(2):
                send_b(p, da, d).wait_recv()
                go(forward_b(p, da, d))
    for p in range(3):
        for db in (3, 1):
            select(p, db)
    for p in range(3):
        relay(p, 0)
    for p in range(3):
        for da in (0, 3, 1, 2):
            for d in range(2):
                forward_b(p, da, d).wait_recv()
        select(p, 2)
    for db in (3, 1, 2):
        for p in range(3):
            relay(p, db)
    for p in range(3):
        for db in range(4):
            for g in range(4):
                cross(p, db, g).wait_recv()
    for copy in weights[3:]:
        copy.wait_recv()
    for copy in started:
        copy.wait_send()
    for copy in local:
        copy.wait()


HBM = pl.BlockSpec(memory_space=pltpu.HBM)


def exchange(tokens, shift, scale, owners, blocks, weights):
    dma = pltpu.SemaphoreType.DMA
    bf16 = jnp.bfloat16
    kv_shape = jax.ShapeDtypeStruct((3, 2, SIDE, SIDE, 8, HALF, PART), bf16)
    table = (N_PB, N_PB * QB_DEV)
    return pl.pallas_call(
        exchange_kernel,
        out_shape=[
            kv_shape,
            jax.ShapeDtypeStruct((8, 128), jnp.int32),
            jax.ShapeDtypeStruct((2, OWN, GRP), bf16),
            jax.ShapeDtypeStruct((4, 2, 2, 2, QBLK, 256), bf16),
        ]
        + [jax.ShapeDtypeStruct(w.shape, w.dtype) for w in weights[1:]],
        in_specs=[HBM] * 11,
        out_specs=[HBM] * 9,
        scratch_shapes=[pltpu.VMEM((SIDE, QB_DEV, HALF, PART), bf16)] * 12
        + [pltpu.VMEM((3, 4, SIDE, 8, HALF, PART), bf16)]
        + [pltpu.VMEM((QB_DEV, HALF, D), bf16)]
        + [pltpu.VMEM((D,), jnp.float32)] * 2
        + [pltpu.VMEM((KT, N_PB * QB_DEV), jnp.int32)] * 2
        + [pltpu.VMEM(table, jnp.int32), pltpu.SMEM(table, jnp.int32)]
        + [pltpu.SMEM((KT, N_PB * QB_DEV), jnp.int32), pltpu.SMEM((8, 128), jnp.int32)]
        + [
            pltpu.VMEM((OWN, D), bf16),
            pltpu.VMEM((3, 2, D, GRP), bf16),
            pltpu.VMEM((2, OWN, GRP), bf16),
            pltpu.VMEM((4, 2, 2, 2, QBLK, 256), bf16),
        ]
        + [dma((3, 2))] * 4
        + [dma((3, 4, 2))] * 4
        + [dma((3, 4, 4))] * 4
        + [dma((3, 4))]
        + [dma((6,))] * 2
        + [dma((QB_DEV,)), dma((15,))],
        compiler_params=pltpu.CompilerParams(
            collective_id=0, has_side_effects=True, vmem_limit_bytes=62 * MIB
        ),
        name="exchange",
    )(tokens, shift, scale, owners, blocks, *weights)


def block_kernel(count_ref, place_ref, *refs):
    vectors_h = refs[0:4]
    tokens_ref, q_h, mine_h, kv_ref = refs[4:8]
    own_h, other_h = refs[8:13], refs[13:18]
    out_ref = refs[18]
    vectors = refs[19:23]
    x_refs = refs[23:25]
    key_refs = refs[25:27]
    value_refs = refs[27:29]
    tok, queries, mine, att = refs[29:33]
    held = refs[33:38]
    wk, wv, wo, w1, w2 = held
    sem, vsem, gsem = refs[38:]
    gate_a, shift_m, scale_m, gate_m = vectors
    bf16 = jnp.bfloat16

    def row(vector):
        return vector[...].reshape(1, D)

    ha = lax.axis_index("ha")
    tokens_in = pltpu.make_async_copy(
        tokens_ref.at[pl.ds(pl.multiple_of(ha * OWN, OWN), OWN)], tok, vsem.at[4]
    )
    q_in = pltpu.make_async_copy(q_h, queries, vsem.at[5])
    mine_in = pltpu.make_async_copy(mine_h, mine, vsem.at[6])
    small = [pltpu.make_async_copy(vectors_h[i], vectors[i], vsem.at[i]) for i in range(4)]
    loads = []
    for i in range(5):
        loads.append(
            (
                pltpu.make_async_copy(own_h[i], held[i].at[ha], sem.at[i]),
                pltpu.make_async_copy(other_h[i], held[i].at[1 - ha], sem.at[5 + i]),
            )
        )

    def begin(*numbers):
        for i in numbers:
            loads[i][0].start()
            loads[i][1].start()

    def ready(*numbers):
        for i in numbers:
            loads[i][0].wait()
            loads[i][1].wait()

    def gathers(blk, slot, act):
        for j in range(KT):
            for p in range(3):
                act(
                    pltpu.make_async_copy(
                        kv_ref.at[p, :, place_ref[p, blk * KT + j]],
                        x_refs[slot].at[j, :, :, pl.ds(p * PART, PART)],
                        gsem.at[slot, j, p],
                    )
                )

    begin(0, 1)
    gathers(0, 0, lambda c: c.start())
    mine_in.start()

    lane = lax.broadcasted_iota(jnp.int32, (QBLK, 256), 1)

    def project(blk, slot):
        x = x_refs[slot][...].reshape(KT * QBLK, D)
        live = count_ref[ha * 4 + blk] * QBLK
        place = lax.broadcasted_iota(jnp.int32, (KT * QBLK, 128), 0)
        bias = jnp.where(place < live, 0.0, DEAD).astype(bf16)
        for g in range(2):
            k = jnp.dot(x, wk[g], preferred_element_type=jnp.float32).astype(bf16)
            v = jnp.dot(x, wv[g], preferred_element_type=jnp.float32).astype(bf16)
            for w, (lo, _, spare) in enumerate(WINDOWS):
                key_refs[slot][g, w, QBLK:, :] = with_lane(k[:, lo : lo + 256], spare, bias)
                value_refs[slot][g, w, QBLK:, :] = with_lane(v[:, lo : lo + 256], spare, jnp.ones_like(bias))
                key_refs[slot][g, w, :QBLK, :] = mine[blk, g, w, 0]
                value_refs[slot][g, w, :QBLK, :] = mine[blk, g, w, 1]

    def attend(blk, slot):
        base = pl.multiple_of(blk * QBLK, QBLK)
        for g in range(2):
            parts = []
            for w, (lo, heads, spare) in enumerate(WINDOWS):
                q = queries[g, pl.ds(base, QBLK), lo : lo + 256]
                masks = [(lane >= h * HDIM - lo) & (lane < (h + 1) * HDIM - lo) for h in heads]
                fixed = jnp.where(lane == spare, jnp.ones_like(q), jnp.zeros_like(q))
                stacked = jnp.concatenate([jnp.where(m, q, fixed) for m in masks], 0)
                scores = lax.dot_general(
                    stacked, key_refs[slot][g, w], (((1,), (1,)), ((), ())), preferred_element_type=jnp.float32
                )
                top = jnp.max(scores, -1, keepdims=True)
                weights = jnp.exp2(scores - top).astype(bf16)
                outs = jnp.dot(weights, value_refs[slot][g, w], preferred_element_type=jnp.float32)
                totals = outs[:, spare : spare + 1]
                above = jnp.zeros((QBLK, 256), jnp.float32)
                below = jnp.ones((QBLK, 256), jnp.float32)
                for i, m in enumerate(masks):
                    rows = slice(i * QBLK, (i + 1) * QBLK)
                    above = jnp.where(m, outs[rows], above)
                    below = jnp.where(m, totals[rows], below)
                parts.append(above / below)
            middle = jnp.where(lane[:, :128] + 128 < 5 * HDIM, parts[0][:, 128:], parts[1][:, :128])
            att[g, pl.ds(base, QBLK), :] = jnp.concatenate(
                [parts[0][:, :128], middle, parts[1][:, 128:]], 1
            ).astype(bf16)

    ready(0, 1)
    mine_in.wait()
    gathers(0, 0, lambda c: c.wait())
    q_in.start()
    gathers(1, 1, lambda c: c.start())
    for copy in small:
        copy.start()
    tokens_in.start()
    begin(2, 3, 4)
    project(0, 0)
    q_in.wait()
    for blk in range(4):
        slot = blk % 2
        if blk < 2:
            gathers(blk + 2, slot, lambda c: c.start())
        if blk < 3:
            gathers(blk + 1, 1 - slot, lambda c: c.wait())
            project(blk + 1, 1 - slot)
        attend(blk, slot)

    for copy in small:
        copy.wait()
    tokens_in.wait()
    ready(2)
    projected = jnp.dot(att[0], wo[0], preferred_element_type=jnp.float32)
    projected += jnp.dot(att[1], wo[1], preferred_element_type=jnp.float32)
    residual = (tok[...].astype(jnp.float32) + row(gate_a) * projected).astype(bf16)
    normed = modulate(residual.astype(jnp.float32), row(shift_m), row(scale_m)).astype(bf16)
    ready(3, 4)
    expanded = jnp.zeros((OWN, D), jnp.float32)
    for g in range(2):
        for lo in range(0, FF // 2, CHUNK):
            hidden = jnp.dot(normed, w1[g, :, lo : lo + CHUNK], preferred_element_type=jnp.float32)
            hidden = jax.nn.gelu(hidden, approximate=True).astype(bf16)
            expanded += jnp.dot(hidden, w2[g, lo : lo + CHUNK, :], preferred_element_type=jnp.float32)
    out_ref[...] = (residual.astype(jnp.float32) + row(gate_m) * expanded).astype(bf16)


def block(counts, places, vectors, tokens, queries, mine, kv, own, other):
    bf16 = jnp.bfloat16
    dma = pltpu.SemaphoreType.DMA
    kv = kv.reshape(3, 2, N_PB * 2, HALF, PART)
    return pl.pallas_call(
        block_kernel,
        out_shape=jax.ShapeDtypeStruct((OWN, D), bf16),
        in_specs=[pl.BlockSpec(memory_space=pltpu.SMEM)] * 2 + [HBM] * 18,
        out_specs=pl.BlockSpec(memory_space=pltpu.VMEM),
        scratch_shapes=[pltpu.VMEM((D,), jnp.float32)] * 4
        + [pltpu.VMEM((KT, 2, HALF, D), bf16)] * 2
        + [pltpu.VMEM((2, 2, ROWS, 256), bf16)] * 4
        + [
            pltpu.VMEM((OWN, D), bf16),
            pltpu.VMEM((2, OWN, GRP), bf16),
            pltpu.VMEM((4, 2, 2, 2, QBLK, 256), bf16),
            pltpu.VMEM((2, OWN, GRP), bf16),
        ]
        + [pltpu.VMEM((2,) + w.shape, bf16) for w in own]
        + [dma((10,)), dma((7,)), dma((2, KT, 3))],
        compiler_params=pltpu.CompilerParams(vmem_limit_bytes=62 * MIB),
        name="block",
    )(counts, places, *vectors, tokens, queries, mine, kv, *own, *other)


def shards(
    tokens,
    shift_attn,
    scale_attn,
    gate_attn,
    shift_mlp,
    scale_mlp,
    gate_mlp,
    w_query,
    w_key,
    w_value,
    w_out,
    w_fc1,
    w_fc2,
    contact_owner,
    contact_local,
    contact_count,
):
    vectors = (gate_attn, shift_mlp, scale_mlp, gate_mlp)
    own = (w_query, w_key, w_value, w_out, w_fc1, w_fc2)
    owners, blocks = contact_owner.T, contact_local.T
    kv, places, queries, mine, *other = exchange(tokens, shift_attn, scale_attn, owners, blocks, own)
    return block(contact_count, places, vectors, tokens, queries, mine, kv, own[1:], other)


def solution(mesh):
    placed = (
        P("pb", None),
        P(),
        P(),
        P(),
        P(),
        P(),
        P(),
        P(None, "ha"),
        P(None, "ha"),
        P(None, "ha"),
        P("ha", None),
        P(None, "ha"),
        P("ha", None),
        P(),
        P(),
        P("pb"),
    )
    return jax.shard_map(
        shards, mesh=mesh, in_specs=placed, out_specs=P(("pb", "ha"), None), check_vma=False
    )
```

time: 158 us -> 152 us (0.962)
  Pallas kernels: 158 us -> 152 us
    pallas_call x1, Pallas kernels: 47.4 us -> 41.1 us  [block(): pl.pallas_call(block_kernel, out_shape=jax.ShapeDtypeStruct((OWN, D), bf1...]
where the time goes in v3:
time: 152 us
  Pallas kernels  152 us (100%)
    pallas_call x1, Pallas kernels, exchange(): pl.pallas_call(exchange_kernel, out_shape=[kv_shape, jax.ShapeDtypeStruct...  111 us
    pallas_call x1, Pallas kernels, block(): pl.pallas_call(block_kernel, out_shape=jax.ShapeDtypeStruct((OWN, D), bf1...  41.1 us

profile of v3, /device:TPU:1, one launch (start us, length us, event | category | flops | bytes accessed | tf_op | source)
XLA Modules:
  0.0 151.9 jit_solution(7602349108664750959)
XLA Ops:
  0.0 110.6 %exchange.1 = (bf16[3,2,4,4,8,64,256]{6,5,4,3,2,1,0:T(8,128)(2,1)}, s32[8,128]{1,0:T(8,128)}, bf16[2,512,384]{2,1,0:T(8,128)(2,1)}, bf16[4,2,2,2,128,256]{5,4,3,...) custom-call(bf16[1024,768]{1,0:T(8,128)(2,1)} %refs_4_.3, ...), custom_call_target="tpu_custom_call" | custom-call | tf_op jit(solution)/shard_map/exchange/pallas_call | solution.py:349
  110.6 41.1 %block.1 = bf16[512,768]{1,0:T(8,128)(2,1)} custom-call(s32[8]{0:T(128)} %count_ref.1, s32[8,128]{1,0:T(8,128)} %get-tuple-element.14.place_ref, f32[768]{0:T(1024)} %refs_0_.3, f32[768]{0:T(1024)} %refs_1_.3, f32[768]{0:T(1024)} %refs_2_.3, f32[768]{0:T(1024)} %refs_3_.3, bf16[1024,768]{1,0:T(8,128)(2,1)} %refs_4_.3, ...), custom_call_target="tpu_custom_call" | custom-call | tf_op jit(solution)/shard_map/block/pallas_call | solution.py:532

commit v4 on v3

--- a/solution.py
+++ b/solution.py
@@ -33,7 +33,7 @@
     return center * lax.rsqrt(spread + epsilon) * (1.0 + scale) + shift
 
 
-ROWS = (1 + KT) * QBLK
+ROWS = KT * QBLK
 OWN = 4 * QBLK
 SHARP = HDIM**-0.5 * 1.4426950408889634
 WINDOWS = ((0, (0, 1, 2, 3, 4), 255), (128, (5, 6, 7), 0))
@@ -51,15 +51,48 @@
     return jnp.concatenate([left, right], 1)
 
 
+def attend_windows(q, keys, values, biased):
+    lane = lax.broadcasted_iota(jnp.int32, (QBLK, 256), 1)
+    found = []
+    for w, (lo, heads, spare) in enumerate(WINDOWS):
+        q_part = q[:, lo : lo + 256]
+        masks = [(lane >= h * HDIM - lo) & (lane < (h + 1) * HDIM - lo) for h in heads]
+        fixed = jnp.zeros_like(q_part)
+        if biased:
+            fixed = jnp.where(lane == spare, jnp.ones_like(q_part), fixed)
+        stacked = jnp.concatenate([jnp.where(m, q_part, fixed) for m in masks], 0)
+        scores = lax.dot_general(
+            stacked, keys[w], (((1,), (1,)), ((), ())), preferred_element_type=jnp.float32
+        )
+        top = jnp.max(scores, -1, keepdims=True)
+        weights = jnp.exp2(scores - top).astype(jnp.bfloat16)
+        outs = jnp.dot(weights, values[w], preferred_element_type=jnp.float32)
+        totals = outs[:, spare : spare + 1]
+        above = jnp.zeros((QBLK, 256), jnp.float32)
+        below = jnp.ones((QBLK, 256), jnp.float32)
+        tops = jnp.zeros((QBLK, 256), jnp.float32)
+        for i, m in enumerate(masks):
+            rows = slice(i * QBLK, (i + 1) * QBLK)
+            above = jnp.where(m, outs[rows], above)
+            below = jnp.where(m, totals[rows], below)
+            tops = jnp.where(m, top[rows], tops)
+        found.append((above, below, tops))
+    use_first = lane[:, :128] + 128 < 5 * HDIM
+    return [
+        jnp.concatenate([one[:, :128], jnp.where(use_first, one[:, 128:], two[:, :128]), two[:, 128:]], 1)
+        for one, two in zip(*found)
+    ]
+
+
 def exchange_kernel(tokens_ref, shift_ref, scale_ref, owner_ref, block_ref, *refs):
     w_in = refs[0:6]
-    kv_ref, place_out, q_out, mine_out = refs[6:10]
-    w_out = refs[10:15]
-    rows = [refs[15 + 4 * p : 19 + 4 * p] for p in range(3)]
-    picked = refs[27]
-    tok, shift, scale, owners, blocks, table, sel_ref, owner_s, places = refs[28:37]
-    own, qkv_w, queries, mine = refs[37:41]
-    (a_s, a_r, af_s, af_r, b_s, b_r, bf_s, bf_r, c_s, c_r, x_s, x_r, l_s, w_s, w_r, t_s, v_s) = refs[41:]
+    kv_ref, place_out, q_out, part_out, log_out = refs[6:11]
+    w_out = refs[11:16]
+    rows = [refs[16 + 4 * p : 20 + 4 * p] for p in range(3)]
+    picked = refs[28]
+    tok, shift, scale, owners, blocks, table, sel_ref, owner_s, places = refs[29:38]
+    own, qkv_w, queries, mine, partial, logs = refs[38:44]
+    (a_s, a_r, af_s, af_r, b_s, b_r, bf_s, bf_r, c_s, c_r, x_s, x_r, l_s, w_s, w_r, t_s, v_s) = refs[44:]
 
     pb = lax.axis_index("pb")
     ha = lax.axis_index("ha")
@@ -110,12 +143,15 @@
     pl.semaphore_signal(barrier, 1, device_id=other, device_id_type=MESH)
     small[0].wait()
     small[1].wait()
-    for t in range(QB_DEV):
+    def norm_tile(t):
         half_rows[t].wait()
         n = modulate(tok[t].astype(jnp.float32), shift[...].reshape(1, D), scale[...].reshape(1, D))
         n = n.astype(jnp.bfloat16)
         for p in range(3):
             rows[p][0][0, t] = n[:, p * PART : (p + 1) * PART]
+
+    for t in range(4):
+        norm_tile(t)
     pl.semaphore_wait(barrier, 10)
 
     started = []
@@ -126,10 +162,15 @@
 
     local = []
 
-    def send_a(p, d):
+    def send_a(p, d, h):
         a = ORDERS[p][0]
+        part = pl.ds(4 * h, 4)
         return remote(
-            rows[p][0].at[0], rows[p][0].at[3 if d == 0 else 1], a_s.at[p, d], a_r.at[p, d], chip(a, 1 if d == 0 else 3)
+            rows[p][0].at[0, part],
+            rows[p][0].at[3 if d == 0 else 1, part],
+            a_s.at[p, d, h],
+            a_r.at[p, d, h],
+            chip(a, 1 if d == 0 else 3),
         )
 
     def forward_a(p, d):
@@ -209,9 +250,13 @@
             send_c(p, db, g).wait_recv()
             go(cross(p, db, g))
 
-    for p in range(3):
-        for d in range(2):
-            go(send_a(p, d))
+    for h in range(2):
+        if h == 1:
+            for t in range(4, QB_DEV):
+                norm_tile(t)
+        for p in range(3):
+            for d in range(2):
+                go(send_a(p, d, h))
     for p in range(3):
         for d in range(2):
             go(send_b(p, 0, d))
@@ -277,24 +322,39 @@
             queries[g] = (product(0) * SHARP).astype(jnp.bfloat16)
             for i in range(2):
                 result = product(1 + i).astype(jnp.bfloat16)
-                fill = jnp.full((QBLK, 128), float(i), jnp.bfloat16)
                 for w, (lo, _, spare) in enumerate(WINDOWS):
-                    for blk in range(4):
-                        mine[blk, g, w, i] = with_lane(
-                            result[blk * QBLK : (blk + 1) * QBLK, lo : lo + 256], spare, fill
-                        )
+                    window = result[:, lo : lo + 256]
+                    if i == 1:
+                        window = with_lane(window, spare, jnp.ones((OWN, 128), jnp.bfloat16))
+                    mine[g, w, i] = window
             return carry
 
         lax.fori_loop(0, 2, one_group, 0)
         keep_local(queries, q_out, 12)
-        keep_local(mine, mine_out, 13)
         lax.fori_loop(0, 4 * KT, place_entry, 0)
         keep_local(places, place_out, 14)
 
+    def own_attention():
+        def one_block(i, carry):
+            g = i // 4
+            at = pl.ds(pl.multiple_of((i % 4) * QBLK, QBLK), QBLK)
+            above, below, tops = attend_windows(
+                queries[g, at, :], [mine[g, w, 0, at, :] for w in range(2)], [mine[g, w, 1, at, :] for w in range(2)], False
+            )
+            partial[g, at, :] = above / below
+            logs[g, at, :] = tops + jnp.log2(below)
+            return carry
+
+        lax.fori_loop(0, 8, one_block, 0)
+        keep_local(partial, part_out, 13)
+        keep_local(logs, log_out, 15)
+
     for p in range(3):
         for d in range(2):
-            send_a(p, d).wait_recv()
+            send_a(p, d, d).wait_recv()
             go(forward_a(p, d))
+        for d in range(2):
+            send_a(p, d, 1 - d).wait_recv()
         for d in range(2):
             for da in (3, 1):
                 go(send_b(p, da, d))
@@ -316,6 +376,7 @@
     for p in range(3):
         for db in (3, 1):
             select(p, db)
+    own_attention()
     for p in range(3):
         relay(p, 0)
     for p in range(3):
@@ -352,11 +413,12 @@
             kv_shape,
             jax.ShapeDtypeStruct((8, 128), jnp.int32),
             jax.ShapeDtypeStruct((2, OWN, GRP), bf16),
-            jax.ShapeDtypeStruct((4, 2, 2, 2, QBLK, 256), bf16),
+            jax.ShapeDtypeStruct((2, OWN, GRP), jnp.float32),
+            jax.ShapeDtypeStruct((2, OWN, GRP), jnp.float32),
         ]
         + [jax.ShapeDtypeStruct(w.shape, w.dtype) for w in weights[1:]],
         in_specs=[HBM] * 11,
-        out_specs=[HBM] * 9,
+        out_specs=[HBM] * 10,
         scratch_shapes=[pltpu.VMEM((SIDE, QB_DEV, HALF, PART), bf16)] * 12
         + [pltpu.VMEM((3, 4, SIDE, 8, HALF, PART), bf16)]
         + [pltpu.VMEM((QB_DEV, HALF, D), bf16)]
@@ -368,14 +430,17 @@
             pltpu.VMEM((OWN, D), bf16),
             pltpu.VMEM((3, 2, D, GRP), bf16),
             pltpu.VMEM((2, OWN, GRP), bf16),
-            pltpu.VMEM((4, 2, 2, 2, QBLK, 256), bf16),
+            pltpu.VMEM((2, 2, 2, OWN, 256), bf16),
+            pltpu.VMEM((2, OWN, GRP), jnp.float32),
+            pltpu.VMEM((2, OWN, GRP), jnp.float32),
         ]
-        + [dma((3, 2))] * 4
+        + [dma((3, 2, 2))] * 2
+        + [dma((3, 2))] * 2
         + [dma((3, 4, 2))] * 4
         + [dma((3, 4, 4))] * 4
         + [dma((3, 4))]
         + [dma((6,))] * 2
-        + [dma((QB_DEV,)), dma((15,))],
+        + [dma((QB_DEV,)), dma((16,))],
         compiler_params=pltpu.CompilerParams(
             collective_id=0, has_side_effects=True, vmem_limit_bytes=62 * MIB
         ),
@@ -385,17 +450,16 @@
 
 def block_kernel(count_ref, place_ref, *refs):
     vectors_h = refs[0:4]
-    tokens_ref, q_h, mine_h, kv_ref = refs[4:8]
-    own_h, other_h = refs[8:13], refs[13:18]
-    out_ref = refs[18]
-    vectors = refs[19:23]
-    x_refs = refs[23:25]
-    key_refs = refs[25:27]
-    value_refs = refs[27:29]
-    tok, queries, mine, att = refs[29:33]
-    held = refs[33:38]
-    wk, wv, wo, w1, w2 = held
-    sem, vsem, gsem = refs[38:]
+    tokens_ref, q_h, part_h, log_h, kv_ref = refs[4:9]
+    own_h, other_h = refs[9:14], refs[14:19]
+    out_ref = refs[19]
+    vectors = refs[20:24]
+    x_refs = refs[24:26]
+    key_refs = refs[26:28]
+    value_refs = refs[28:30]
+    tok, queries, partial, logs, att = refs[30:35]
+    wkv, wo, w1, w2 = refs[35:39]
+    sem, vsem, gsem = refs[39:]
     gate_a, shift_m, scale_m, gate_m = vectors
     bf16 = jnp.bfloat16
 
@@ -403,20 +467,29 @@
         return vector[...].reshape(1, D)
 
     ha = lax.axis_index("ha")
-    tokens_in = pltpu.make_async_copy(
-        tokens_ref.at[pl.ds(pl.multiple_of(ha * OWN, OWN), OWN)], tok, vsem.at[4]
-    )
-    q_in = pltpu.make_async_copy(q_h, queries, vsem.at[5])
-    mine_in = pltpu.make_async_copy(mine_h, mine, vsem.at[6])
-    small = [pltpu.make_async_copy(vectors_h[i], vectors[i], vsem.at[i]) for i in range(4)]
+    late = [
+        pltpu.make_async_copy(src, dst, vsem.at[i])
+        for i, (src, dst) in enumerate(
+            [(vectors_h[i], vectors[i]) for i in range(4)]
+            + [(tokens_ref.at[pl.ds(pl.multiple_of(ha * OWN, OWN), OWN)], tok)]
+        )
+    ]
+    early = [
+        pltpu.make_async_copy(src, dst, vsem.at[5 + i])
+        for i, (src, dst) in enumerate(((q_h, queries), (part_h, partial), (log_h, logs)))
+    ]
     loads = []
     for i in range(5):
-        loads.append(
-            (
-                pltpu.make_async_copy(own_h[i], held[i].at[ha], sem.at[i]),
-                pltpu.make_async_copy(other_h[i], held[i].at[1 - ha], sem.at[5 + i]),
-            )
-        )
+        pair = []
+        for src, at, number in ((own_h[i], ha, i), (other_h[i], 1 - ha, 5 + i)):
+            if i < 2:
+                dst = wkv.at[at, :, pl.ds(i * GRP, GRP)]
+            elif i == 2:
+                dst = wo.at[pl.ds(pl.multiple_of(at * GRP, GRP), GRP)]
+            else:
+                dst = (w1, w2)[i - 3].at[at]
+            pair.append(pltpu.make_async_copy(src, dst, sem.at[number]))
+        loads.append(pair)
 
     def begin(*numbers):
         for i in numbers:
@@ -439,65 +512,46 @@
                     )
                 )
 
+    def project(blk, slot):
+        x = x_refs[slot][...].reshape(ROWS, D)
+        live = count_ref[ha * 4 + blk] * QBLK
+        place = lax.broadcasted_iota(jnp.int32, (ROWS, 128), 0)
+        bias = jnp.where(place < live, 0.0, DEAD).astype(bf16)
+        for g in range(2):
+            both = jnp.dot(x, wkv[g], preferred_element_type=jnp.float32).astype(bf16)
+            k, v = both[:, :GRP], both[:, GRP:]
+            for w, (lo, _, spare) in enumerate(WINDOWS):
+                key_refs[slot][g, w] = with_lane(k[:, lo : lo + 256], spare, bias)
+                value_refs[slot][g, w] = with_lane(v[:, lo : lo + 256], spare, jnp.ones_like(bias))
+
+    def attend(blk, slot):
+        at = slice(blk * QBLK, (blk + 1) * QBLK)
+        for g in range(2):
+            above, below, tops = attend_windows(
+                queries[g, at, :],
+                [key_refs[slot].at[g, w][...] for w in range(2)],
+                [value_refs[slot].at[g, w][...] for w in range(2)],
+                True,
+            )
+            log = logs[g, at, :]
+            most = jnp.maximum(tops, log)
+            listed, mine = jnp.exp2(tops - most), jnp.exp2(log - most)
+            result = (above * listed + partial[g, at, :] * mine) / (below * listed + mine)
+            att[at, g * GRP : (g + 1) * GRP] = result.astype(bf16)
+
     begin(0, 1)
     gathers(0, 0, lambda c: c.start())
-    mine_in.start()
-
-    lane = lax.broadcasted_iota(jnp.int32, (QBLK, 256), 1)
-
-    def project(blk, slot):
-        x = x_refs[slot][...].reshape(KT * QBLK, D)
-        live = count_ref[ha * 4 + blk] * QBLK
-        place = lax.broadcasted_iota(jnp.int32, (KT * QBLK, 128), 0)
-        bias = jnp.where(place < live, 0.0, DEAD).astype(bf16)
-        for g in range(2):
-            k = jnp.dot(x, wk[g], preferred_element_type=jnp.float32).astype(bf16)
-            v = jnp.dot(x, wv[g], preferred_element_type=jnp.float32).astype(bf16)
-            for w, (lo, _, spare) in enumerate(WINDOWS):
-                key_refs[slot][g, w, QBLK:, :] = with_lane(k[:, lo : lo + 256], spare, bias)
-                value_refs[slot][g, w, QBLK:, :] = with_lane(v[:, lo : lo + 256], spare, jnp.ones_like(bias))
-                key_refs[slot][g, w, :QBLK, :] = mine[blk, g, w, 0]
-                value_refs[slot][g, w, :QBLK, :] = mine[blk, g, w, 1]
-
-    def attend(blk, slot):
-        base = pl.multiple_of(blk * QBLK, QBLK)
-        for g in range(2):
-            parts = []
-            for w, (lo, heads, spare) in enumerate(WINDOWS):
-                q = queries[g, pl.ds(base, QBLK), lo : lo + 256]
-                masks = [(lane >= h * HDIM - lo) & (lane < (h + 1) * HDIM - lo) for h in heads]
-                fixed = jnp.where(lane == spare, jnp.ones_like(q), jnp.zeros_like(q))
-                stacked = jnp.concatenate([jnp.where(m, q, fixed) for m in masks], 0)
-                scores = lax.dot_general(
-                    stacked, key_refs[slot][g, w], (((1,), (1,)), ((), ())), preferred_element_type=jnp.float32
-                )
-                top = jnp.max(scores, -1, keepdims=True)
-                weights = jnp.exp2(scores - top).astype(bf16)
-                outs = jnp.dot(weights, value_refs[slot][g, w], preferred_element_type=jnp.float32)
-                totals = outs[:, spare : spare + 1]
-                above = jnp.zeros((QBLK, 256), jnp.float32)
-                below = jnp.ones((QBLK, 256), jnp.float32)
-                for i, m in enumerate(masks):
-                    rows = slice(i * QBLK, (i + 1) * QBLK)
-                    above = jnp.where(m, outs[rows], above)
-                    below = jnp.where(m, totals[rows], below)
-                parts.append(above / below)
-            middle = jnp.where(lane[:, :128] + 128 < 5 * HDIM, parts[0][:, 128:], parts[1][:, :128])
-            att[g, pl.ds(base, QBLK), :] = jnp.concatenate(
-                [parts[0][:, :128], middle, parts[1][:, 128:]], 1
-            ).astype(bf16)
-
     ready(0, 1)
-    mine_in.wait()
     gathers(0, 0, lambda c: c.wait())
-    q_in.start()
+    for copy in early:
+        copy.start()
     gathers(1, 1, lambda c: c.start())
-    for copy in small:
+    for copy in late:
         copy.start()
-    tokens_in.start()
     begin(2, 3, 4)
     project(0, 0)
-    q_in.wait()
+    for copy in early:
+        copy.wait()
     for blk in range(4):
         slot = blk % 2
         if blk < 2:
@@ -507,12 +561,10 @@
             project(blk + 1, 1 - slot)
         attend(blk, slot)
 
-    for copy in small:
+    for copy in late:
         copy.wait()
-    tokens_in.wait()
     ready(2)
-    projected = jnp.dot(att[0], wo[0], preferred_element_type=jnp.float32)
-    projected += jnp.dot(att[1], wo[1], preferred_element_type=jnp.float32)
+    projected = jnp.dot(att[...], wo[...], preferred_element_type=jnp.float32)
     residual = (tok[...].astype(jnp.float32) + row(gate_a) * projected).astype(bf16)
     normed = modulate(residual.astype(jnp.float32), row(shift_m), row(scale_m)).astype(bf16)
     ready(3, 4)
@@ -525,14 +577,14 @@
     out_ref[...] = (residual.astype(jnp.float32) + row(gate_m) * expanded).astype(bf16)
 
 
-def block(counts, places, vectors, tokens, queries, mine, kv, own, other):
+def block(counts, places, vectors, tokens, queries, partial, logs, kv, own, other):
     bf16 = jnp.bfloat16
     dma = pltpu.SemaphoreType.DMA
     kv = kv.reshape(3, 2, N_PB * 2, HALF, PART)
     return pl.pallas_call(
         block_kernel,
         out_shape=jax.ShapeDtypeStruct((OWN, D), bf16),
-        in_specs=[pl.BlockSpec(memory_space=pltpu.SMEM)] * 2 + [HBM] * 18,
+        in_specs=[pl.BlockSpec(memory_space=pltpu.SMEM)] * 2 + [HBM] * 19,
         out_specs=pl.BlockSpec(memory_space=pltpu.VMEM),
         scratch_shapes=[pltpu.VMEM((D,), jnp.float32)] * 4
         + [pltpu.VMEM((KT, 2, HALF, D), bf16)] * 2
@@ -540,14 +592,18 @@
         + [
             pltpu.VMEM((OWN, D), bf16),
             pltpu.VMEM((2, OWN, GRP), bf16),
-            pltpu.VMEM((4, 2, 2, 2, QBLK, 256), bf16),
-            pltpu.VMEM((2, OWN, GRP), bf16),
+            pltpu.VMEM((2, OWN, GRP), jnp.float32),
+            pltpu.VMEM((2, OWN, GRP), jnp.float32),
+            pltpu.VMEM((OWN, D), bf16),
+            pltpu.VMEM((2, D, 2 * GRP), bf16),
+            pltpu.VMEM((D, D), bf16),
+            pltpu.VMEM((2, D, FF // 2), bf16),
+            pltpu.VMEM((2, FF // 2, D), bf16),
         ]
-        + [pltpu.VMEM((2,) + w.shape, bf16) for w in own]
-        + [dma((10,)), dma((7,)), dma((2, KT, 3))],
+        + [dma((10,)), dma((8,)), dma((2, KT, 3))],
         compiler_params=pltpu.CompilerParams(vmem_limit_bytes=62 * MIB),
         name="block",
-    )(counts, places, *vectors, tokens, queries, mine, kv, *own, *other)
+    )(counts, places, *vectors, tokens, queries, partial, logs, kv, *own, *other)
 
 
 def shards(
@@ -571,8 +627,8 @@
     vectors = (gate_attn, shift_mlp, scale_mlp, gate_mlp)
     own = (w_query, w_key, w_value, w_out, w_fc1, w_fc2)
     owners, blocks = contact_owner.T, contact_local.T
-    kv, places, queries, mine, *other = exchange(tokens, shift_attn, scale_attn, owners, blocks, own)
-    return block(contact_count, places, vectors, tokens, queries, mine, kv, own[1:], other)
+    kv, places, queries, partial, logs, *other = exchange(tokens, shift_attn, scale_attn, owners, blocks, own)
+    return block(contact_count, places, vectors, tokens, queries, partial, logs, kv, own[1:], other)
 
 
 def solution(mesh):

time: 152 us -> 146 us (0.961)
  Pallas kernels: 152 us -> 146 us
    pallas_call x1, Pallas kernels: 41.1 us -> 34.2 us  [block(): pl.pallas_call(block_kernel, out_shape=jax.ShapeDtypeStruct((OWN, D), bf1...]
where the time goes in v4:
time: 146 us
  Pallas kernels  146 us (100%)
    pallas_call x1, Pallas kernels, exchange(): pl.pallas_call(exchange_kernel, out_shape=[kv_shape, jax.ShapeDtypeStruct...  112 us
    pallas_call x1, Pallas kernels, block(): pl.pallas_call(block_kernel, out_shape=jax.ShapeDtypeStruct((OWN, D), bf1...  34.2 us

profile of v4, /device:TPU:1, one launch (start us, length us, event | category | flops | bytes accessed | tf_op | source)
XLA Modules:
  0.0 146.1 jit_solution(18094220263655130116)
XLA Ops:
  0.0 111.7 %exchange.1 = (bf16[3,2,4,4,8,64,256]{6,5,4,3,2,1,0:T(8,128)(2,1)}, s32[8,128]{1,0:T(8,128)}, bf16[2,512,384]{2,1,0:T(8,128)(2,1)}, f32[2,512,384]{2,1,0:T(8,128...) custom-call(bf16[1024,768]{1,0:T(8,128)(2,1)} %refs_4_.3, ...), custom_call_target="tpu_custom_call" | custom-call | tf_op jit(solution)/shard_map/exchange/pallas_call | solution.py:410
  111.7 34.2 %block.1 = bf16[512,768]{1,0:T(8,128)(2,1)} custom-call(s32[8]{0:T(128)} %count_ref.1, s32[8,128]{1,0:T(8,128)} %get-tuple-element.15.place_ref, f32[768]{0:T(1024)} %refs_0_.3, f32[768]{0:T(1024)} %refs_1_.3, f32[768]{0:T(1024)} %refs_2_.3, f32[768]{0:T(1024)} %refs_3_.3, bf16[1024,768]{1,0:T(8,128)(2,1)} %refs_4_.3, ...), custom_call_target="tpu_custom_call" | custom-call | tf_op jit(solution)/shard_map/block/pallas_call | solution.py:584

commit v5 on v4

--- a/solution.py
+++ b/solution.py
@@ -92,7 +92,7 @@
     picked = refs[28]
     tok, shift, scale, owners, blocks, table, sel_ref, owner_s, places = refs[29:38]
     own, qkv_w, queries, mine, partial, logs = refs[38:44]
-    (a_s, a_r, af_s, af_r, b_s, b_r, bf_s, bf_r, c_s, c_r, x_s, x_r, l_s, w_s, w_r, t_s, v_s) = refs[44:]
+    (a_s, a_r, af_s, af_r, b_s, b_r, bf_s, bf_r, c_s, c_r, last_r, x_s, x_r, l_s, w_s, w_r, t_s, v_s) = refs[44:]
 
     pb = lax.axis_index("pb")
     ha = lax.axis_index("ha")
@@ -111,12 +111,9 @@
             src_ref=src, dst_ref=dst, send_sem=ssem, recv_sem=rsem, device_id=dev, device_id_type=MESH
         )
 
-    half_rows = [
-        pltpu.make_async_copy(
-            tokens_ref.at[pl.ds(pl.multiple_of(t * QBLK + ha * HALF, HALF), HALF)], tok.at[t], t_s.at[t]
-        )
-        for t in range(QB_DEV)
-    ]
+    half_rows = pltpu.make_async_copy(
+        tokens_ref.at[:, pl.ds(pl.multiple_of(ha * HALF, HALF), HALF)], tok, t_s
+    )
     small = [
         pltpu.make_async_copy(src, dst, v_s.at[i])
         for i, (src, dst) in enumerate(
@@ -126,14 +123,14 @@
                 (owner_ref, owners),
                 (block_ref, blocks),
                 (owner_ref, owner_s),
-                (tokens_ref.at[pl.ds(pl.multiple_of(ha * OWN, OWN), OWN)], own),
+                (tokens_ref.at[pl.ds(ha * 4, 4)], own),
                 (w_in[0], qkv_w.at[0, ha]),
                 (w_in[1], qkv_w.at[1, ha]),
                 (w_in[2], qkv_w.at[2, ha]),
             )
         )
     ]
-    for copy in small[:2] + half_rows + small[2:]:
+    for copy in small[:2] + [half_rows] + small[2:]:
         copy.start()
 
     barrier = pltpu.get_barrier_semaphore()
@@ -143,33 +140,29 @@
     pl.semaphore_signal(barrier, 1, device_id=other, device_id_type=MESH)
     small[0].wait()
     small[1].wait()
-    def norm_tile(t):
-        half_rows[t].wait()
+    half_rows.wait()
+    for t in range(QB_DEV):
         n = modulate(tok[t].astype(jnp.float32), shift[...].reshape(1, D), scale[...].reshape(1, D))
         n = n.astype(jnp.bfloat16)
         for p in range(3):
             rows[p][0][0, t] = n[:, p * PART : (p + 1) * PART]
-
-    for t in range(4):
-        norm_tile(t)
     pl.semaphore_wait(barrier, 10)
-
-    started = []
 
     def go(copy):
         copy.start()
-        started.append(copy)
+
+    def arrived(ref, semaphore):
+        remote(ref, ref, x_s, semaphore, other).wait_recv()
 
     local = []
 
-    def send_a(p, d, h):
+    def send_a(p, d):
         a = ORDERS[p][0]
-        part = pl.ds(4 * h, 4)
         return remote(
-            rows[p][0].at[0, part],
-            rows[p][0].at[3 if d == 0 else 1, part],
-            a_s.at[p, d, h],
-            a_r.at[p, d, h],
+            rows[p][0].at[0],
+            rows[p][0].at[3 if d == 0 else 1],
+            a_s,
+            a_r.at[p, d],
             chip(a, 1 if d == 0 else 3),
         )
 
@@ -179,8 +172,8 @@
         return remote(
             rows[p][0].at[3 if d == 0 else 1, part],
             rows[p][0].at[2, part],
-            af_s.at[p, d],
-            af_r.at[p, d],
+            af_s,
+            af_r.at[p],
             chip(a, 1 if d == 0 else 3),
         )
 
@@ -189,7 +182,7 @@
         return remote(
             rows[p][0].at[da],
             rows[p][3 if d == 0 else 1].at[da],
-            b_s.at[p, da, d],
+            b_s,
             b_r.at[p, da, d],
             chip(b, 1 if d == 0 else 3),
         )
@@ -200,8 +193,8 @@
         return remote(
             rows[p][3 if d == 0 else 1].at[da, part],
             rows[p][2].at[da, part],
-            bf_s.at[p, da, d],
-            bf_r.at[p, da, d],
+            bf_s,
+            bf_r.at[p],
             chip(b, 1 if d == 0 else 3),
         )
 
@@ -211,19 +204,17 @@
         return remote(
             picked.at[p, g, db],
             kv_ref.at[p, 0, SIDE - off, db],
-            c_s.at[p, db, g],
-            c_r.at[p, db, g],
+            c_s,
+            last_r.at[p, g - 1] if db == 2 else c_r.at[p, db],
             chip(c, off),
         )
 
     def cross(p, db, g):
         src = picked.at[p, 0, db] if g == 0 else kv_ref.at[p, 0, SIDE - OFFS[g], db]
-        return remote(
-            src, kv_ref.at[p, 1, (SIDE - OFFS[g]) % SIDE, db], x_s.at[p, db, g], x_r.at[p, db, g], other
-        )
+        return remote(src, kv_ref.at[p, 1, (SIDE - OFFS[g]) % SIDE, db], x_s, x_r, other)
 
     def keep(p, db):
-        return pltpu.make_async_copy(picked.at[p, 0, db], kv_ref.at[p, 0, 0, db], l_s.at[p, db])
+        return pltpu.make_async_copy(picked.at[p, 0, db], kv_ref.at[p, 0, 0, db], l_s)
 
     def select(p, db):
         a, b, c = ORDERS[p]
@@ -241,22 +232,20 @@
             lax.fori_loop(0, 8, pick, 0)
         for g in (3, 1, 2):
             go(send_c(p, db, g))
-        local.append(keep(p, db))
-        local[-1].start()
+        keep(p, db).start()
         go(cross(p, db, 0))
 
-    def relay(p, db):
-        for g in (1, 2, 3):
-            send_c(p, db, g).wait_recv()
+    def relay(p, db, *groups):
+        if db != 2:
+            arrived(kv_ref.at[p, 0, pl.ds(1, 3), db], c_r.at[p, db])
+        for g in groups:
+            if db == 2:
+                send_c(p, db, g).wait_recv()
             go(cross(p, db, g))
 
-    for h in range(2):
-        if h == 1:
-            for t in range(4, QB_DEV):
-                norm_tile(t)
-        for p in range(3):
-            for d in range(2):
-                go(send_a(p, d, h))
+    for p in range(3):
+        for d in range(2):
+            go(send_a(p, d))
     for p in range(3):
         for d in range(2):
             go(send_b(p, 0, d))
@@ -266,29 +255,6 @@
     ]
     for copy in weights:
         go(copy)
-
-    small[2].wait()
-    small[3].wait()
-    lane = lax.broadcasted_iota(jnp.int32, (KT, N_PB * QB_DEV), 1)
-    order = (lane & 7) * KT + lax.broadcasted_iota(jnp.int32, (KT, N_PB * QB_DEV), 0)
-    code = order * 8 + blocks[...]
-    size = N_PB * QB_DEV
-
-    def tabulate(o, carry):
-        hit = owners[...] == o
-        first = jnp.where(hit, code, 511)
-        last = jnp.where(hit, code, 0)
-        for step in (1, 2, 4):
-            first = jnp.minimum(first, pltpu.roll(first, size - step, 1))
-            last = jnp.maximum(last, pltpu.roll(last, size - step, 1))
-        first = jnp.min(first, 0, keepdims=True)
-        last = jnp.max(last, 0, keepdims=True)
-        table[pl.ds(o, 1), :] = first + (last & 7) * 512
-        return carry
-
-    lax.fori_loop(0, N_PB, tabulate, 0)
-    to_scalars = pltpu.make_async_copy(table, sel_ref, v_s.at[9])
-    to_scalars.start()
 
     def keep_local(src, dst, number):
         local.append(pltpu.make_async_copy(src, dst, v_s.at[number]))
@@ -307,8 +273,9 @@
 
     def own_blocks():
         small[5].wait()
-        normed = modulate(own[...].astype(jnp.float32), shift[...].reshape(1, D), scale[...].reshape(1, D))
-        own[...] = normed.astype(jnp.bfloat16)
+        stream = own[...].reshape(OWN, D).astype(jnp.float32)
+        normed = modulate(stream, shift[...].reshape(1, D), scale[...].reshape(1, D))
+        own[...] = normed.astype(jnp.bfloat16).reshape(4, QBLK, D)
         for i in range(3):
             small[6 + i].wait()
             remote(w_in[i], qkv_w.at[i, 1 - ha], w_s.at[i], w_r.at[i], other).wait_recv()
@@ -317,7 +284,9 @@
 
         def one_group(g, carry):
             def product(i):
-                return jnp.dot(own[...], qkv_w[i, g], preferred_element_type=jnp.float32)
+                return jnp.dot(
+                    own[...].reshape(OWN, D), qkv_w[i, g], preferred_element_type=jnp.float32
+                )
 
             queries[g] = (product(0) * SHARP).astype(jnp.bfloat16)
             for i in range(2):
@@ -351,23 +320,43 @@
 
     for p in range(3):
         for d in range(2):
-            send_a(p, d, d).wait_recv()
+            send_a(p, d).wait_recv()
             go(forward_a(p, d))
-        for d in range(2):
-            send_a(p, d, 1 - d).wait_recv()
         for d in range(2):
             for da in (3, 1):
                 go(send_b(p, da, d))
     for p in range(3):
-        for d in range(2):
-            forward_a(p, d).wait_recv()
+        arrived(rows[p][0].at[2], af_r.at[p])
         for d in range(2):
             go(send_b(p, 2, d))
+    small[2].wait()
+    small[3].wait()
+    lane = lax.broadcasted_iota(jnp.int32, (KT, N_PB * QB_DEV), 1)
+    order = (lane & 7) * KT + lax.broadcasted_iota(jnp.int32, (KT, N_PB * QB_DEV), 0)
+    code = order * 8 + blocks[...]
+    size = N_PB * QB_DEV
+
+    def tabulate(i, carry):
+        firsts, lasts = [], []
+        for o in range(8):
+            hit = owners[...] == i * 8 + o
+            firsts.append(jnp.min(jnp.where(hit, code, 511), 0, keepdims=True))
+            lasts.append(jnp.max(jnp.where(hit, code, 0), 0, keepdims=True))
+        first, last = jnp.concatenate(firsts, 0), jnp.concatenate(lasts, 0)
+        for step in (1, 2, 4):
+            first = jnp.minimum(first, pltpu.roll(first, size - step, 1))
+            last = jnp.maximum(last, pltpu.roll(last, size - step, 1))
+        table[pl.ds(pl.multiple_of(i * 8, 8), 8), :] = first + (last & 7) * 512
+        return carry
+
+    lax.fori_loop(0, N_PB // 8, tabulate, 0)
+    to_scalars = pltpu.make_async_copy(table, sel_ref, v_s.at[9])
+    to_scalars.start()
+
     to_scalars.wait()
     small[4].wait()
     for p in range(3):
         select(p, 0)
-    own_blocks()
     for da in (0, 3, 1, 2):
         for p in range(3):
             for d in range(2):
@@ -376,25 +365,35 @@
     for p in range(3):
         for db in (3, 1):
             select(p, db)
+    own_blocks()
     own_attention()
     for p in range(3):
-        relay(p, 0)
-    for p in range(3):
-        for da in (0, 3, 1, 2):
-            for d in range(2):
-                forward_b(p, da, d).wait_recv()
+        relay(p, 0, 1, 2, 3)
+    for p in range(3):
+        arrived(rows[p][2], bf_r.at[p])
         select(p, 2)
-    for db in (3, 1, 2):
+    for db in (3, 1):
         for p in range(3):
-            relay(p, db)
-    for p in range(3):
-        for db in range(4):
-            for g in range(4):
-                cross(p, db, g).wait_recv()
+            relay(p, db, 1, 2, 3)
+    for g in (3, 1, 2):
+        for p in range(3):
+            relay(p, 2, g)
+    arrived(kv_ref.at[:, 1], x_r)
     for copy in weights[3:]:
         copy.wait_recv()
-    for copy in started:
+    for copy in weights:
         copy.wait_send()
+    two, one = pl.ds(0, 2), pl.ds(0, 1)
+    for ref, semaphore in (
+        (kv_ref.at[:, 0, one, two], a_s),
+        (kv_ref.at[:, 0, one, one], af_s),
+        (kv_ref.at[:, 0, two], b_s),
+        (kv_ref.at[:, 0, one], bf_s),
+        (kv_ref.at[:, 0, pl.ds(1, 3)], c_s),
+        (kv_ref.at[:, 1], x_s),
+    ):
+        remote(ref, ref, semaphore, x_r, other).wait_send()
+    pltpu.make_async_copy(picked.at[:, 0], kv_ref.at[:, 0, 0], l_s).wait()
     for copy in local:
         copy.wait()
 
@@ -427,25 +426,22 @@
         + [pltpu.VMEM(table, jnp.int32), pltpu.SMEM(table, jnp.int32)]
         + [pltpu.SMEM((KT, N_PB * QB_DEV), jnp.int32), pltpu.SMEM((8, 128), jnp.int32)]
         + [
-            pltpu.VMEM((OWN, D), bf16),
+            pltpu.VMEM((4, QBLK, D), bf16),
             pltpu.VMEM((3, 2, D, GRP), bf16),
             pltpu.VMEM((2, OWN, GRP), bf16),
             pltpu.VMEM((2, 2, 2, OWN, 256), bf16),
             pltpu.VMEM((2, OWN, GRP), jnp.float32),
             pltpu.VMEM((2, OWN, GRP), jnp.float32),
         ]
-        + [dma((3, 2, 2))] * 2
-        + [dma((3, 2))] * 2
-        + [dma((3, 4, 2))] * 4
-        + [dma((3, 4, 4))] * 4
-        + [dma((3, 4))]
-        + [dma((6,))] * 2
-        + [dma((QB_DEV,)), dma((16,))],
+        + [dma, dma((3, 2)), dma, dma((3,))]
+        + [dma, dma((3, 4, 2)), dma, dma((3,))]
+        + [dma, dma((3, 4)), dma((3, 3)), dma, dma, dma]
+        + [dma((6,)), dma((6,)), dma, dma((16,))],
         compiler_params=pltpu.CompilerParams(
             collective_id=0, has_side_effects=True, vmem_limit_bytes=62 * MIB
         ),
         name="exchange",
-    )(tokens, shift, scale, owners, blocks, *weights)
+    )(tokens.reshape(QB_DEV, QBLK, D), shift, scale, owners, blocks, *weights)
 
 
 def block_kernel(count_ref, place_ref, *refs):
@@ -501,16 +497,17 @@
             loads[i][0].wait()
             loads[i][1].wait()
 
-    def gathers(blk, slot, act):
+    def gather(blk, slot):
         for j in range(KT):
             for p in range(3):
-                act(
-                    pltpu.make_async_copy(
-                        kv_ref.at[p, :, place_ref[p, blk * KT + j]],
-                        x_refs[slot].at[j, :, :, pl.ds(p * PART, PART)],
-                        gsem.at[slot, j, p],
-                    )
-                )
+                pltpu.make_async_copy(
+                    kv_ref.at[p, :, place_ref[p, blk * KT + j]],
+                    x_refs[slot].at[j, :, :, pl.ds(p * PART, PART)],
+                    gsem.at[slot],
+                ).start()
+
+    def gathered(slot):
+        pltpu.make_async_copy(x_refs[slot], x_refs[slot], gsem.at[slot]).wait()
 
     def project(blk, slot):
         x = x_refs[slot][...].reshape(ROWS, D)
@@ -540,12 +537,12 @@
             att[at, g * GRP : (g + 1) * GRP] = result.astype(bf16)
 
     begin(0, 1)
-    gathers(0, 0, lambda c: c.start())
+    gather(0, 0)
     ready(0, 1)
-    gathers(0, 0, lambda c: c.wait())
+    gathered(0)
     for copy in early:
         copy.start()
-    gathers(1, 1, lambda c: c.start())
+    gather(1, 1)
     for copy in late:
         copy.start()
     begin(2, 3, 4)
@@ -555,9 +552,9 @@
     for blk in range(4):
         slot = blk % 2
         if blk < 2:
-            gathers(blk + 2, slot, lambda c: c.start())
+            gather(blk + 2, slot)
         if blk < 3:
-            gathers(blk + 1, 1 - slot, lambda c: c.wait())
+            gathered(1 - slot)
             project(blk + 1, 1 - slot)
         attend(blk, slot)
 
@@ -600,7 +597,7 @@
             pltpu.VMEM((2, D, FF // 2), bf16),
             pltpu.VMEM((2, FF // 2, D), bf16),
         ]
-        + [dma((10,)), dma((8,)), dma((2, KT, 3))],
+        + [dma((10,)), dma((8,)), dma((2,))],
         compiler_params=pltpu.CompilerParams(vmem_limit_bytes=62 * MIB),
         name="block",
     )(counts, places, *vectors, tokens, queries, partial, logs, kv, *own, *other)

time: 146 us -> 138 us (0.945)
  Pallas kernels: 146 us -> 138 us
    pallas_call x1, Pallas kernels: 112 us -> 104 us  [exchange(): pl.pallas_call(exchange_kernel, out_shape=[kv_shape, jax.ShapeDtypeStruct...]
where the time goes in v5:
time: 138 us
  Pallas kernels  138 us (100%)
    pallas_call x1, Pallas kernels, exchange(): pl.pallas_call(exchange_kernel, out_shape=[kv_shape, jax.ShapeDtypeStruct...  104 us
    pallas_call x1, Pallas kernels, block(): pl.pallas_call(block_kernel, out_shape=jax.ShapeDtypeStruct((OWN, D), bf1...  33.7 us

profile of v5, /device:TPU:1, one launch (start us, length us, event | category | flops | bytes accessed | tf_op | source)
XLA Modules:
  0.0 138.1 jit_solution(450653752971914738)
XLA Ops:
  0.0 104.2 %exchange.1 = (bf16[3,2,4,4,8,64,256]{6,5,4,3,2,1,0:T(8,128)(2,1)}, s32[8,128]{1,0:T(8,128)}, bf16[2,512,384]{2,1,0:T(8,128)(2,1)}, f32[2,512,384]{2,1,0:T(8,128...) custom-call(bf16[8,128,768]{2,1,0:T(8,128)(2,1)} %bitcast.5, ...), custom_call_target="tpu_custom_call" | custom-call | tf_op jit(solution)/shard_map/exchange/pallas_call | solution.py:409
  104.2 33.7 %block.1 = bf16[512,768]{1,0:T(8,128)(2,1)} custom-call(s32[8]{0:T(128)} %count_ref.1, s32[8,128]{1,0:T(8,128)} %get-tuple-element.15.place_ref, f32[768]{0:T(1024)} %refs_0_.3, f32[768]{0:T(1024)} %refs_1_.3, f32[768]{0:T(1024)} %refs_2_.3, f32[768]{0:T(1024)} %refs_3_.3, bf16[1024,768]{1,0:T(8,128)(2,1)} %refs_4_.3, ...), custom_call_target="tpu_custom_call" | custom-call | tf_op jit(solution)/shard_map/block/pallas_call | solution.py:581

commit v6 on v5

--- a/solution.py
+++ b/solution.py
@@ -23,6 +23,11 @@
 ORDERS = ((2, 1, 0), (1, 0, 2), (0, 2, 1))
 STRIDES = (16, 4, 1)
 OFFS = (0, 1, 3, 2)
+
+CAP = 22
+PIECES = 2
+PIECE = CAP // PIECES
+SLOTS = -(-CAP // 8) * 8
 
 epsilon = 1e-06
 
@@ -444,6 +449,365 @@
     )(tokens.reshape(QB_DEV, QBLK, D), shift, scale, owners, blocks, *weights)
 
 
+def pooled_kernel(tokens_ref, shift_ref, scale_ref, owner_ref, block_ref, *refs):
+    w_in = refs[0:6]
+    kv_ref, place_out, q_out, part_out, log_out, most_out = refs[6:12]
+    w_out = refs[12:17]
+    plane = refs[17:20]
+    picked = refs[20]
+    tok, shift, scale, owners, blocks, table, sel_ref, ranks, rank_s, owner_s, places, most = refs[21:33]
+    own, qkv_w, queries, mine, partial, logs = refs[33:39]
+    (a_s, a_r, af_s, af_r, b_s, b_r, bf_s, bf_r, c_s, c_r, x_s, x_r, l_s, w_s, w_r, t_s, v_s) = refs[39:]
+
+    pb = lax.axis_index("pb")
+    ha = lax.axis_index("ha")
+    me = (pb // 16, (pb // 4) % 4, pb % 4)
+
+    def moved(base, axis, off):
+        return base + (lax.rem(me[axis] + off, SIDE) - me[axis]) * STRIDES[axis]
+
+    def chip(axis, off):
+        return {"pb": moved(pb, axis, off), "ha": ha}
+
+    other = {"pb": pb, "ha": 1 - ha}
+
+    def remote(src, dst, ssem, rsem, dev):
+        return pltpu.make_async_remote_copy(
+            src_ref=src, dst_ref=dst, send_sem=ssem, recv_sem=rsem, device_id=dev, device_id_type=MESH
+        )
+
+    half_rows = pltpu.make_async_copy(
+        tokens_ref.at[:, pl.ds(pl.multiple_of(ha * HALF, HALF), HALF)], tok, t_s
+    )
+    small = [
+        pltpu.make_async_copy(src, dst, v_s.at[i])
+        for i, (src, dst) in enumerate(
+            (
+                (shift_ref, shift),
+                (scale_ref, scale),
+                (owner_ref, owners),
+                (block_ref, blocks),
+                (owner_ref, owner_s),
+                (tokens_ref.at[pl.ds(ha * 4, 4)], own),
+                (w_in[0], qkv_w.at[0, ha]),
+                (w_in[1], qkv_w.at[1, ha]),
+                (w_in[2], qkv_w.at[2, ha]),
+            )
+        )
+    ]
+    for copy in small[:2] + [half_rows] + small[2:]:
+        copy.start()
+
+    barrier = pltpu.get_barrier_semaphore()
+    for axis in range(3):
+        for off in (1, 2, 3):
+            pl.semaphore_signal(barrier, 1, device_id=chip(axis, off), device_id_type=MESH)
+    pl.semaphore_signal(barrier, 1, device_id=other, device_id_type=MESH)
+    small[0].wait()
+    small[1].wait()
+    half_rows.wait()
+    for t in range(QB_DEV):
+        n = modulate(tok[t].astype(jnp.float32), shift[...].reshape(1, D), scale[...].reshape(1, D))
+        n = n.astype(jnp.bfloat16)
+        for p in range(3):
+            plane[p][t] = n[:, p * PART : (p + 1) * PART]
+    pl.semaphore_wait(barrier, 10)
+
+    def go(copy):
+        copy.start()
+
+    def arrived(ref, semaphore):
+        remote(ref, ref, x_s, semaphore, other).wait_recv()
+
+    local = []
+
+    def tiles(p, db, da, first=0, count=QB_DEV):
+        return plane[p].at[pl.ds((db * SIDE + da) * QB_DEV + first, count)]
+
+    def send_a(p, d):
+        return remote(
+            tiles(p, 0, 0), tiles(p, 0, 3 if d == 0 else 1), a_s, a_r.at[p, d], chip(ORDERS[p][0], 1 if d == 0 else 3)
+        )
+
+    def forward_a(p, d):
+        return remote(
+            tiles(p, 0, 3 if d == 0 else 1, 4 * d, 4),
+            tiles(p, 0, 2, 4 * d, 4),
+            af_s,
+            af_r.at[p],
+            chip(ORDERS[p][0], 1 if d == 0 else 3),
+        )
+
+    def send_b(p, da, d):
+        return remote(
+            tiles(p, 0, da),
+            tiles(p, 3 if d == 0 else 1, da),
+            b_s,
+            b_r.at[p, da, d],
+            chip(ORDERS[p][1], 1 if d == 0 else 3),
+        )
+
+    def forward_b(p, da, d):
+        return remote(
+            tiles(p, 3 if d == 0 else 1, da, 4 * d, 4),
+            tiles(p, 2, da, 4 * d, 4),
+            bf_s,
+            bf_r.at[p],
+            chip(ORDERS[p][1], 1 if d == 0 else 3),
+        )
+
+    def send_c(p, g, h):
+        off = OFFS[g]
+        return remote(
+            picked.at[p, g, pl.ds(h * PIECE, PIECE)],
+            kv_ref.at[p, 0, SIDE - off, pl.ds(h * PIECE, PIECE)],
+            c_s,
+            c_r.at[p, g - 1, h],
+            chip(ORDERS[p][2], off),
+        )
+
+    def cross(p, g, h):
+        part = pl.ds(h * PIECE, PIECE)
+        src = picked.at[p, 0, part] if g == 0 else kv_ref.at[p, 0, SIDE - OFFS[g], part]
+        return remote(src, kv_ref.at[p, 1, (SIDE - OFFS[g]) % SIDE, part], x_s, x_r, other)
+
+    def select(p, g, h):
+        lane = moved(pb, ORDERS[p][2], OFFS[g]) * QB_DEV
+
+        def pick(i, carry):
+            at = h * PIECE + i
+            picked[p, g, at] = plane[p][sel_ref[p, at, lane]]
+            return carry
+
+        lax.fori_loop(0, PIECE, pick, 0, unroll=PIECE)
+
+    for p in range(3):
+        for d in range(2):
+            go(send_a(p, d))
+    for p in range(3):
+        for d in range(2):
+            go(send_b(p, 0, d))
+    weights = [
+        remote(w_in[i], qkv_w.at[i, ha] if i < 3 else w_out[i - 1], w_s.at[i], w_r.at[i], other)
+        for i in range(6)
+    ]
+    for copy in weights:
+        go(copy)
+
+    def keep_local(src, dst, number):
+        local.append(pltpu.make_async_copy(src, dst, v_s.at[number]))
+        local[-1].start()
+
+    def place_entry(e, carry):
+        i, j = e // KT, e % KT
+        at = pb * QB_DEV + ha * 4 + i
+        owner = owner_s[j, at]
+        for p in range(3):
+            c = ORDERS[p][2]
+            rel = (owner // STRIDES[c] - me[c]) & 3
+            places[p, e] = rel * SIDE * 8 + jnp.minimum(rank_s[c, j, at], CAP - 1)
+        return carry
+
+    def own_blocks():
+        small[5].wait()
+        stream = own[...].reshape(OWN, D).astype(jnp.float32)
+        normed = modulate(stream, shift[...].reshape(1, D), scale[...].reshape(1, D))
+        own[...] = normed.astype(jnp.bfloat16).reshape(4, QBLK, D)
+        for i in range(3):
+            small[6 + i].wait()
+            remote(w_in[i], qkv_w.at[i, 1 - ha], w_s.at[i], w_r.at[i], other).wait_recv()
+        keep_local(qkv_w.at[1, 1 - ha], w_out[0], 16)
+        keep_local(qkv_w.at[2, 1 - ha], w_out[1], 11)
+
+        def one_group(g, carry):
+            def product(i):
+                return jnp.dot(
+                    own[...].reshape(OWN, D), qkv_w[i, g], preferred_element_type=jnp.float32
+                )
+
+            queries[g] = (product(0) * SHARP).astype(jnp.bfloat16)
+            for i in range(2):
+                result = product(1 + i).astype(jnp.bfloat16)
+                for w, (lo, _, spare) in enumerate(WINDOWS):
+                    window = result[:, lo : lo + 256]
+                    if i == 1:
+                        window = with_lane(window, spare, jnp.ones((OWN, 128), jnp.bfloat16))
+                    mine[g, w, i] = window
+            return carry
+
+        lax.fori_loop(0, 2, one_group, 0)
+        keep_local(queries, q_out, 12)
+        lax.fori_loop(0, 4 * KT, place_entry, 0)
+        keep_local(places, place_out, 14)
+
+    def own_attention():
+        def one_block(i, carry):
+            g = i // 4
+            at = pl.ds(pl.multiple_of((i % 4) * QBLK, QBLK), QBLK)
+            above, below, tops = attend_windows(
+                queries[g, at, :], [mine[g, w, 0, at, :] for w in range(2)], [mine[g, w, 1, at, :] for w in range(2)], False
+            )
+            partial[g, at, :] = above / below
+            logs[g, at, :] = tops + jnp.log2(below)
+            return carry
+
+        lax.fori_loop(0, 8, one_block, 0)
+        keep_local(partial, part_out, 13)
+        keep_local(logs, log_out, 15)
+
+    for p in range(3):
+        for d in range(2):
+            send_a(p, d).wait_recv()
+            go(forward_a(p, d))
+        for d in range(2):
+            for da in (3, 1):
+                go(send_b(p, da, d))
+    for p in range(3):
+        arrived(tiles(p, 0, 2), af_r.at[p])
+        for d in range(2):
+            go(send_b(p, 2, d))
+    small[2].wait()
+    small[3].wait()
+    size = N_PB * QB_DEV
+    wide = (KT, size)
+    lane = lax.broadcasted_iota(jnp.int32, wide, 1) & 7
+    line = lax.broadcasted_iota(jnp.int32, wide, 0)
+    coords = [(owners[...] // stride) & 3 for stride in STRIDES]
+
+    def ranked(marks):
+        column = marks
+        for step in (1, 2, 4):
+            column = column + jnp.where(line >= step, pltpu.roll(column, step, 0), 0)
+        total = jnp.broadcast_to(jnp.sum(marks, 0, keepdims=True), wide)
+        row = total
+        for step in (1, 2, 4):
+            row = row + jnp.where(lane >= step, pltpu.roll(row, step, 1), 0)
+        return column - marks + row - total
+
+    top = jnp.zeros(wide, jnp.int32)
+    for axis in range(3):
+        rank = jnp.zeros(wide, jnp.int32)
+        for value in range(SIDE):
+            here = coords[axis] == value
+            rank = jnp.where(here, ranked(here.astype(jnp.int32)), rank)
+        ranks[axis] = rank
+        top = jnp.maximum(top, rank)
+    most[...] = jnp.broadcast_to(jnp.max(jnp.max(top, 1, keepdims=True), 0, keepdims=True), (8, 128))
+
+    for p in range(3):
+        a, b, c = ORDERS[p]
+        rel_b, rel_a = (coords[b] - me[b]) & 3, (coords[a] - me[a]) & 3
+        number = (rel_b * SIDE + rel_a) * QB_DEV + blocks[...]
+        slot = jnp.where(coords[c] == me[c], ranks[c], -1)
+
+        def tabulate(i, carry):
+            found = [
+                jnp.max(jnp.where(slot == i * 8 + n, number, 0), 0, keepdims=True) for n in range(8)
+            ]
+            found = jnp.concatenate(found, 0)
+            for step in (1, 2, 4):
+                found = jnp.maximum(found, pltpu.roll(found, size - step, 1))
+            table[p, pl.ds(pl.multiple_of(i * 8, 8), 8), :] = found
+            return carry
+
+        lax.fori_loop(0, SLOTS // 8, tabulate, 0)
+    to_scalars = pltpu.make_async_copy(table, sel_ref, v_s.at[9])
+    to_scalars.start()
+    ranks_out = pltpu.make_async_copy(ranks, rank_s, v_s.at[10])
+    ranks_out.start()
+    for da in (0, 3, 1, 2):
+        for p in range(3):
+            for d in range(2):
+                send_b(p, da, d).wait_recv()
+                go(forward_b(p, da, d))
+    to_scalars.wait()
+    ranks_out.wait()
+    small[4].wait()
+    keep_local(most, most_out, 17)
+    own_blocks()
+    for p in range(3):
+        arrived(plane[p].at[pl.ds(2 * SIDE * QB_DEV, SIDE * QB_DEV)], bf_r.at[p])
+        for h in range(PIECES):
+            for g in (3, 1, 2):
+                select(p, g, h)
+                go(send_c(p, g, h))
+    for p in range(3):
+        for h in range(PIECES):
+            select(p, 0, h)
+            go(cross(p, 0, h))
+        pltpu.make_async_copy(picked.at[p, 0], kv_ref.at[p, 0, 0, pl.ds(0, CAP)], l_s).start()
+    own_attention()
+    for h in range(PIECES):
+        for g in (3, 1, 2):
+            for p in range(3):
+                send_c(p, g, h).wait_recv()
+                go(cross(p, g, h))
+    arrived(kv_ref.at[:, 1, :, pl.ds(0, CAP)], x_r)
+    for copy in weights[3:]:
+        copy.wait_recv()
+    for copy in weights:
+        copy.wait_send()
+    for ref, semaphore in (
+        (kv_ref.at[:, 0, pl.ds(0, 2), pl.ds(0, 8)], a_s),
+        (kv_ref.at[:, 0, pl.ds(0, 1), pl.ds(0, 8)], af_s),
+        (kv_ref.at[:, 0, :, pl.ds(0, 16)], b_s),
+        (kv_ref.at[:, 0, :, pl.ds(0, 8)], bf_s),
+        (picked.at[:, pl.ds(1, 3)], c_s),
+        (kv_ref.at[:, 1, :, pl.ds(0, CAP)], x_s),
+    ):
+        remote(ref, ref, semaphore, x_r, other).wait_send()
+    pltpu.make_async_copy(picked.at[:, 0], kv_ref.at[:, 0, 0, pl.ds(0, CAP)], l_s).wait()
+    for copy in local:
+        copy.wait()
+
+
+def exchange_pooled(tokens, shift, scale, owners, blocks, weights):
+    dma = pltpu.SemaphoreType.DMA
+    bf16 = jnp.bfloat16
+    kv_shape = jax.ShapeDtypeStruct((3, 2, SIDE, SIDE * 8, HALF, PART), bf16)
+    table = (3, SLOTS, N_PB * QB_DEV)
+    ranks = (3, KT, N_PB * QB_DEV)
+    return pl.pallas_call(
+        pooled_kernel,
+        out_shape=[
+            kv_shape,
+            jax.ShapeDtypeStruct((8, 128), jnp.int32),
+            jax.ShapeDtypeStruct((2, OWN, GRP), bf16),
+            jax.ShapeDtypeStruct((2, OWN, GRP), jnp.float32),
+            jax.ShapeDtypeStruct((2, OWN, GRP), jnp.float32),
+            jax.ShapeDtypeStruct((8, 128), jnp.int32),
+        ]
+        + [jax.ShapeDtypeStruct(w.shape, w.dtype) for w in weights[1:]],
+        in_specs=[HBM] * 11,
+        out_specs=[HBM] * 11,
+        scratch_shapes=[pltpu.VMEM((SIDE * SIDE * QB_DEV, HALF, PART), bf16)] * 3
+        + [pltpu.VMEM((3, 4, CAP, HALF, PART), bf16)]
+        + [pltpu.VMEM((QB_DEV, HALF, D), bf16)]
+        + [pltpu.VMEM((D,), jnp.float32)] * 2
+        + [pltpu.VMEM((KT, N_PB * QB_DEV), jnp.int32)] * 2
+        + [pltpu.VMEM(table, jnp.int32), pltpu.SMEM(table, jnp.int32)]
+        + [pltpu.VMEM(ranks, jnp.int32), pltpu.SMEM(ranks, jnp.int32)]
+        + [pltpu.SMEM((KT, N_PB * QB_DEV), jnp.int32), pltpu.SMEM((8, 128), jnp.int32)]
+        + [pltpu.VMEM((8, 128), jnp.int32)]
+        + [
+            pltpu.VMEM((4, QBLK, D), bf16),
+            pltpu.VMEM((3, 2, D, GRP), bf16),
+            pltpu.VMEM((2, OWN, GRP), bf16),
+            pltpu.VMEM((2, 2, 2, OWN, 256), bf16),
+            pltpu.VMEM((2, OWN, GRP), jnp.float32),
+            pltpu.VMEM((2, OWN, GRP), jnp.float32),
+        ]
+        + [dma, dma((3, 2)), dma, dma((3,))]
+        + [dma, dma((3, 4, 2)), dma, dma((3,))]
+        + [dma, dma((3, 3, PIECES)), dma, dma, dma]
+        + [dma((6,)), dma((6,)), dma, dma((18,))],
+        compiler_params=pltpu.CompilerParams(
+            collective_id=1, has_side_effects=True, vmem_limit_bytes=62 * MIB
+        ),
+        name="exchange_pooled",
+    )(tokens.reshape(QB_DEV, QBLK, D), shift, scale, owners, blocks, *weights)
+
+
 def block_kernel(count_ref, place_ref, *refs):
     vectors_h = refs[0:4]
     tokens_ref, q_h, part_h, log_h, kv_ref = refs[4:9]
@@ -577,7 +941,7 @@
 def block(counts, places, vectors, tokens, queries, partial, logs, kv, own, other):
     bf16 = jnp.bfloat16
     dma = pltpu.SemaphoreType.DMA
-    kv = kv.reshape(3, 2, N_PB * 2, HALF, PART)
+    kv = kv.reshape(3, 2, -1, HALF, PART)
     return pl.pallas_call(
         block_kernel,
         out_shape=jax.ShapeDtypeStruct((OWN, D), bf16),
@@ -624,8 +988,15 @@
     vectors = (gate_attn, shift_mlp, scale_mlp, gate_mlp)
     own = (w_query, w_key, w_value, w_out, w_fc1, w_fc2)
     owners, blocks = contact_owner.T, contact_local.T
-    kv, places, queries, partial, logs, *other = exchange(tokens, shift_attn, scale_attn, owners, blocks, own)
-    return block(contact_count, places, vectors, tokens, queries, partial, logs, kv, own[1:], other)
+    args = (tokens, shift_attn, scale_attn, owners, blocks, own)
+    kv, places, queries, partial, logs, most, *other = exchange_pooled(*args)
+
+    def crowded():
+        other_kv, other_places, *_ = exchange(*args)
+        return other_kv.reshape(kv.shape), other_places
+
+    kv_used, places_used = lax.cond(most[0, 0] < CAP, lambda: (kv, places), crowded)
+    return block(contact_count, places_used, vectors, tokens, queries, partial, logs, kv_used, own[1:], other)
 
 
 def solution(mesh):

time: 138 us -> 127 us (0.920)
  Pallas kernels: 138 us -> 125 us
    pallas_call x1, Pallas kernels: 104 us -> 91.2 us  [exchange_pooled(): pl.pallas_call(pooled_kernel, out_shape=[kv_shape, jax.ShapeDtypeStruct((...]
where the time goes in v6:
time: 127 us
  Pallas kernels  125 us (98%)
    pallas_call x1, Pallas kernels, exchange_pooled(): pl.pallas_call(pooled_kernel, out_shape=[kv_shape, jax.ShapeDtypeStruct((...  91.2 us
    pallas_call x1, Pallas kernels, block(): pl.pallas_call(block_kernel, out_shape=jax.ShapeDtypeStruct((OWN, D), bf1...  33.9 us

profile of v6, /device:TPU:1, one launch (start us, length us, event | category | flops | bytes accessed | tf_op | source)
XLA Modules:
  0.0 127.2 jit_solution(12566496833195924429)
XLA Ops:
  0.0 0.0 copy-start
  0.0 0.0 copy-start.1
  0.0 0.0 copy-start.2
  0.0 0.0 copy-start.3
  0.0 0.0 copy-start.4
  0.0 91.2 %exchange_pooled.1 = (bf16[3,2,4,32,64,256]{5,4,3,2,1,0:T(8,128)(2,1)}, s32[8,128]{1,0:T(8,128)S(1)}, bf16[2,512,384]{2,1,0:T(8,128)(2,1)}, f32[2,512,384]{2,1,0...) custom-call(bf16[8,128,768]{2,1,0:T(8,128)(2,1)} %bitcast.9, ...), custom_call_target="tpu_custom_call" | custom-call | tf_op jit(solution)/shard_map/exchange_pooled/pallas_call | solution.py:770
  91.2 1.2 slice.3
  93.1 0.0 copy-done
  93.1 0.0 copy-done.1
  93.1 0.0 copy-done.2
  93.1 0.0 copy-done.3
  93.1 0.0 copy-done.4
  93.2 33.9 %block.1 = bf16[512,768]{1,0:T(8,128)(2,1)} custom-call(s32[8]{0:T(128)} %count_ref.1, s32[8,128]{1,0:T(8,128)S(1)} %get-tuple-element.65.place_ref, f32[768]{0:T(1024)} %refs_0_.3, f32[768]{0:T(1024)} %refs_1_.3, f32[768]{0:T(1024)} %refs_2_.3, f32[768]{0:T(1024)} %refs_3_.3, bf16[1024,768]{1,0:T(8,128)(2,1)S(1)} %copy-done, ...), custom_call_target="tpu_custom_call" | custom-call | tf_op jit(solution)/shard_map/block/pallas_call | solution.py:945
  (1 shorter events, 0.0 us)
Async XLA Ops:
  0.0 93.1 %copy-start = (bf16[1024,768]{1,0:T(8,128)(2,1)S(1)}, bf16[1024,768]{1,0:T(8,128)(2,1)}, u32[]{:S(2)}) copy-start(bf16[1024,768]{1,0:T(8,128)(2,1)} %refs_4_.3) | copy-start | bytes 4718596
  0.0 93.1 %copy-start.1 = (s32[512,8]{0,1:T(8,128)S(1)}, s32[512,8]{0,1:T(8,128)}, u32[]{:S(2)}) copy-start(s32[512,8]{0,1:T(8,128)} %param.31) | copy-start | bytes 49156
  0.0 93.1 %copy-start.2 = (s32[512,8]{0,1:T(8,128)S(1)}, s32[512,8]{0,1:T(8,128)}, u32[]{:S(2)}) copy-start(s32[512,8]{0,1:T(8,128)} %param.32) | copy-start | bytes 49156
  0.0 93.1 %copy-start.3 = (f32[768]{0:T(1024)S(1)}, f32[768]{0:T(1024)}, u32[]{:S(2)}) copy-start(f32[768]{0:T(1024)} %shift_ref.1) | copy-start | bytes 9220
  0.0 93.1 %copy-start.4 = (f32[768]{0:T(1024)S(1)}, f32[768]{0:T(1024)}, u32[]{:S(2)}) copy-start(f32[768]{0:T(1024)} %scale_ref.1) | copy-start | bytes 9220

commit v7 on v6

--- a/solution.py
+++ b/solution.py
@@ -455,9 +455,9 @@
     w_out = refs[12:17]
     plane = refs[17:20]
     picked = refs[20]
-    tok, shift, scale, owners, blocks, table, sel_ref, ranks, rank_s, owner_s, places, most = refs[21:33]
-    own, qkv_w, queries, mine, partial, logs = refs[33:39]
-    (a_s, a_r, af_s, af_r, b_s, b_r, bf_s, bf_r, c_s, c_r, x_s, x_r, l_s, w_s, w_r, t_s, v_s) = refs[39:]
+    tok, shift, scale, owners, blocks, table, sel_ref, ranks, rank_s, owner_s, places = refs[21:32]
+    own, qkv_w, queries, mine, partial, logs = refs[32:38]
+    (a_s, a_r, af_s, af_r, b_s, b_r, bf_s, bf_r, c_s, c_r, x_s, x_r, l_s, w_s, w_r, t_s, v_s) = refs[38:]
 
     pb = lax.axis_index("pb")
     ha = lax.axis_index("ha")
@@ -692,7 +692,7 @@
             rank = jnp.where(here, ranked(here.astype(jnp.int32)), rank)
         ranks[axis] = rank
         top = jnp.maximum(top, rank)
-    most[...] = jnp.broadcast_to(jnp.max(jnp.max(top, 1, keepdims=True), 0, keepdims=True), (8, 128))
+    most_out[0, 0] = jnp.max(top)
 
     for p in range(3):
         a, b, c = ORDERS[p]
@@ -723,7 +723,6 @@
     to_scalars.wait()
     ranks_out.wait()
     small[4].wait()
-    keep_local(most, most_out, 17)
     own_blocks()
     for p in range(3):
         arrived(plane[p].at[pl.ds(2 * SIDE * QB_DEV, SIDE * QB_DEV)], bf_r.at[p])
@@ -775,11 +774,11 @@
             jax.ShapeDtypeStruct((2, OWN, GRP), bf16),
             jax.ShapeDtypeStruct((2, OWN, GRP), jnp.float32),
             jax.ShapeDtypeStruct((2, OWN, GRP), jnp.float32),
-            jax.ShapeDtypeStruct((8, 128), jnp.int32),
+            jax.ShapeDtypeStruct((1, 1), jnp.int32),
         ]
         + [jax.ShapeDtypeStruct(w.shape, w.dtype) for w in weights[1:]],
         in_specs=[HBM] * 11,
-        out_specs=[HBM] * 11,
+        out_specs=[HBM] * 5 + [pl.BlockSpec(memory_space=pltpu.SMEM)] + [HBM] * 5,
         scratch_shapes=[pltpu.VMEM((SIDE * SIDE * QB_DEV, HALF, PART), bf16)] * 3
         + [pltpu.VMEM((3, 4, CAP, HALF, PART), bf16)]
         + [pltpu.VMEM((QB_DEV, HALF, D), bf16)]
@@ -788,7 +787,6 @@
         + [pltpu.VMEM(table, jnp.int32), pltpu.SMEM(table, jnp.int32)]
         + [pltpu.VMEM(ranks, jnp.int32), pltpu.SMEM(ranks, jnp.int32)]
         + [pltpu.SMEM((KT, N_PB * QB_DEV), jnp.int32), pltpu.SMEM((8, 128), jnp.int32)]
-        + [pltpu.VMEM((8, 128), jnp.int32)]
         + [
             pltpu.VMEM((4, QBLK, D), bf16),
             pltpu.VMEM((3, 2, D, GRP), bf16),
@@ -800,7 +798,7 @@
         + [dma, dma((3, 2)), dma, dma((3,))]
         + [dma, dma((3, 4, 2)), dma, dma((3,))]
         + [dma, dma((3, 3, PIECES)), dma, dma, dma]
-        + [dma((6,)), dma((6,)), dma, dma((18,))],
+        + [dma((6,)), dma((6,)), dma, dma((17,))],
         compiler_params=pltpu.CompilerParams(
             collective_id=1, has_side_effects=True, vmem_limit_bytes=62 * MIB
         ),

time: 127 us -> 127 us (level)
  no operation moved by 1% of the time
where the time goes in v7:
time: 127 us; the launch traced here: 126 us
  Pallas kernels  126 us (99%)
    pallas_call x1, Pallas kernels, exchange_pooled(): pl.pallas_call(pooled_kernel, out_shape=[kv_shape, jax.ShapeDtypeStruct((...  91.8 us
    pallas_call x1, Pallas kernels, block(): pl.pallas_call(block_kernel, out_shape=jax.ShapeDtypeStruct((OWN, D), bf1...  33.9 us

profile of v7, /device:TPU:1, one launch (start us, length us, event | category | flops | bytes accessed | tf_op | source)
XLA Modules:
  0.0 126.4 jit_solution(12975990566361500873)
XLA Ops:
  0.0 0.0 copy-start
  0.0 0.0 copy-start.1
  0.0 0.0 copy-start.2
  0.0 0.0 copy-start.3
  0.0 0.0 copy-start.4
  0.0 91.8 %exchange_pooled.1 = (bf16[3,2,4,32,64,256]{5,4,3,2,1,0:T(8,128)(2,1)}, s32[8,128]{1,0:T(8,128)S(1)}, bf16[2,512,384]{2,1,0:T(8,128)(2,1)}, f32[2,512,384]{2,1,0...) custom-call(bf16[8,128,768]{2,1,0:T(8,128)(2,1)} %bitcast.9, ...), custom_call_target="tpu_custom_call" | custom-call | tf_op jit(solution)/shard_map/exchange_pooled/pallas_call | solution.py:769
  92.3 0.0 copy-done
  92.3 0.0 copy-done.1
  92.4 0.0 copy-done.2
  92.4 0.0 copy-done.3
  92.4 0.0 copy-done.4
  92.4 33.9 %block.1 = bf16[512,768]{1,0:T(8,128)(2,1)} custom-call(s32[8]{0:T(128)} %count_ref.1, s32[8,128]{1,0:T(8,128)S(1)} %get-tuple-element.65.place_ref, f32[768]{0:T(1024)} %refs_0_.3, f32[768]{0:T(1024)} %refs_1_.3, f32[768]{0:T(1024)} %refs_2_.3, f32[768]{0:T(1024)} %refs_3_.3, bf16[1024,768]{1,0:T(8,128)(2,1)S(1)} %copy-done, ...), custom_call_target="tpu_custom_call" | custom-call | tf_op jit(solution)/shard_map/block/pallas_call | solution.py:943
  (1 shorter events, 0.0 us)
Async XLA Ops:
  0.0 92.3 %copy-start = (bf16[1024,768]{1,0:T(8,128)(2,1)S(1)}, bf16[1024,768]{1,0:T(8,128)(2,1)}, u32[]{:S(2)}) copy-start(bf16[1024,768]{1,0:T(8,128)(2,1)} %refs_4_.3) | copy-start | bytes 4718596
  0.0 92.3 %copy-start.1 = (s32[512,8]{0,1:T(8,128)S(1)}, s32[512,8]{0,1:T(8,128)}, u32[]{:S(2)}) copy-start(s32[512,8]{0,1:T(8,128)} %param.31) | copy-start | bytes 49156
  0.0 92.4 %copy-start.2 = (s32[512,8]{0,1:T(8,128)S(1)}, s32[512,8]{0,1:T(8,128)}, u32[]{:S(2)}) copy-start(s32[512,8]{0,1:T(8,128)} %param.32) | copy-start | bytes 49156
  0.0 92.4 %copy-start.3 = (f32[768]{0:T(1024)S(1)}, f32[768]{0:T(1024)}, u32[]{:S(2)}) copy-start(f32[768]{0:T(1024)} %shift_ref.1) | copy-start | bytes 9220
  0.0 92.4 %copy-start.4 = (f32[768]{0:T(1024)S(1)}, f32[768]{0:T(1024)}, u32[]{:S(2)}) copy-start(f32[768]{0:T(1024)} %scale_ref.1) | copy-start | bytes 9220

commit v8 on v7

--- a/solution.py
+++ b/solution.py
@@ -666,6 +666,11 @@
         arrived(tiles(p, 0, 2), af_r.at[p])
         for d in range(2):
             go(send_b(p, 2, d))
+    for da in (0, 3):
+        for p in range(3):
+            for d in range(2):
+                send_b(p, da, d).wait_recv()
+                go(forward_b(p, da, d))
     small[2].wait()
     small[3].wait()
     size = N_PB * QB_DEV
@@ -715,7 +720,7 @@
     to_scalars.start()
     ranks_out = pltpu.make_async_copy(ranks, rank_s, v_s.at[10])
     ranks_out.start()
-    for da in (0, 3, 1, 2):
+    for da in (1, 2):
         for p in range(3):
             for d in range(2):
                 send_b(p, da, d).wait_recv()

time: 127 us -> 127 us (level)
  no operation moved by 1% of the time
where the time goes in v8:
time: 127 us; the launch traced here: 126 us
  Pallas kernels  126 us (99%)
    pallas_call x1, Pallas kernels, exchange_pooled(): pl.pallas_call(pooled_kernel, out_shape=[kv_shape, jax.ShapeDtypeStruct((...  91.8 us
    pallas_call x1, Pallas kernels, block(): pl.pallas_call(block_kernel, out_shape=jax.ShapeDtypeStruct((OWN, D), bf1...  33.9 us

profile of v8, /device:TPU:1, one launch (start us, length us, event | category | flops | bytes accessed | tf_op | source)
XLA Modules:
  0.0 126.4 jit_solution(11964432727640400654)
XLA Ops:
  0.0 0.0 copy-start
  0.0 0.0 copy-start.1
  0.0 0.0 copy-start.2
  0.0 0.0 copy-start.3
  0.0 0.0 copy-start.4
  0.0 91.8 %exchange_pooled.1 = (bf16[3,2,4,32,64,256]{5,4,3,2,1,0:T(8,128)(2,1)}, s32[8,128]{1,0:T(8,128)S(1)}, bf16[2,512,384]{2,1,0:T(8,128)(2,1)}, f32[2,512,384]{2,1,0...) custom-call(bf16[8,128,768]{2,1,0:T(8,128)(2,1)} %bitcast.9, ...), custom_call_target="tpu_custom_call" | custom-call | tf_op jit(solution)/shard_map/exchange_pooled/pallas_call | solution.py:774
  92.3 0.0 copy-done
  92.3 0.0 copy-done.1
  92.4 0.0 copy-done.2
  92.4 0.0 copy-done.3
  92.4 0.0 copy-done.4
  92.4 33.9 %block.1 = bf16[512,768]{1,0:T(8,128)(2,1)} custom-call(s32[8]{0:T(128)} %count_ref.1, s32[8,128]{1,0:T(8,128)S(1)} %get-tuple-element.65.place_ref, f32[768]{0:T(1024)} %refs_0_.3, f32[768]{0:T(1024)} %refs_1_.3, f32[768]{0:T(1024)} %refs_2_.3, f32[768]{0:T(1024)} %refs_3_.3, bf16[1024,768]{1,0:T(8,128)(2,1)S(1)} %copy-done, ...), custom_call_target="tpu_custom_call" | custom-call | tf_op jit(solution)/shard_map/block/pallas_call | solution.py:948
  (1 shorter events, 0.0 us)
Async XLA Ops:
  0.0 92.3 %copy-start = (bf16[1024,768]{1,0:T(8,128)(2,1)S(1)}, bf16[1024,768]{1,0:T(8,128)(2,1)}, u32[]{:S(2)}) copy-start(bf16[1024,768]{1,0:T(8,128)(2,1)} %refs_4_.3) | copy-start | bytes 4718596
  0.0 92.3 %copy-start.1 = (s32[512,8]{0,1:T(8,128)S(1)}, s32[512,8]{0,1:T(8,128)}, u32[]{:S(2)}) copy-start(s32[512,8]{0,1:T(8,128)} %param.31) | copy-start | bytes 49156
  0.0 92.4 %copy-start.2 = (s32[512,8]{0,1:T(8,128)S(1)}, s32[512,8]{0,1:T(8,128)}, u32[]{:S(2)}) copy-start(s32[512,8]{0,1:T(8,128)} %param.32) | copy-start | bytes 49156
  0.0 92.4 %copy-start.3 = (f32[768]{0:T(1024)S(1)}, f32[768]{0:T(1024)}, u32[]{:S(2)}) copy-start(f32[768]{0:T(1024)} %shift_ref.1) | copy-start | bytes 9220
  0.0 92.4 %copy-start.4 = (f32[768]{0:T(1024)S(1)}, f32[768]{0:T(1024)}, u32[]{:S(2)}) copy-start(f32[768]{0:T(1024)} %scale_ref.1) | copy-start | bytes 9220
